TPU v7x, 128 devices: a whole 4x4x4 slice. The times are simulated.
128 devices in a mesh: grp: 8 (over y, core), leaf: 16 (over z, x).
Axes of the slice: x: 4, y: 4, z: 4, core: 2. Of those that a mesh axis runs over, the one named last changes fastest.
Arguments:
- points: float32 [3, 524288], P(None, ('grp', 'leaf')), as said below
- rhs: float32 [8, 524288], P(None, ('grp', 'leaf')), may hold values from -8 to 8
- start: float32 [8, 524288], P(None, ('grp', 'leaf')), may hold values from -0.6 to 0.6
- leaf_skel: float32 [3, 131072], P(None, ('grp', 'leaf')), as said below
- mid_skel: float32 [3, 8192], P(None, ('grp', 'leaf')), as said below
- top_skel: float32 [3, 512], replicated, as said below
- leaf_basis: float32 [2048, 64, 256], P(('grp', 'leaf')), may hold values from -0.375 to 0.375
- leaf_transfer: float32 [2048, 64, 64], P(('grp', 'leaf')), may hold values from -0.75 to 0.75
- mid_transfer: float32 [128, 64, 64], P(('grp', 'leaf')), may hold values from -0.75 to 0.75
- noise: float32 [1], replicated, may hold values from 0.5 to 2
- near: int32 [2048, 16], P(('grp', 'leaf')), may hold values from 0 to 47, as said below
- near_count: int32 [2048], P(('grp', 'leaf')), may hold values from 1 to 16, as said below
- far_leaf: int32 [2048, 32], P(('grp', 'leaf')), may hold values from 0 to 255, as said below
- far_leaf_count: int32 [2048], P(('grp', 'leaf')), may hold values from 1 to 32, as said below
- far_mid: int32 [128, 16], P(('grp', 'leaf')), may hold values from 0 to 127, as said below
- far_top: int32 [8, 3], P('grp'), may hold values from 0 to 7, as said below
Outputs:
- updated: float32 [8, 524288], P(None, ('grp', 'leaf'))
- residual: float32 [8, 524288], P(None, ('grp', 'leaf'))
Inputs may be any that keep to these rules, and one draw needn't show every extreme that they name: `points`: leaves lie in unit boxes on an integer grid in Morton order; every point and skeleton point lies in a box of a leaf of its cluster. `leaf_skel`: skeleton points of a leaf lie in its box. `mid_skel`: skeleton points of a middle cluster lie in boxes of its leaves. `top_skel`: skeleton points of a top cluster lie in boxes of its leaves. `near`: the index j = (l // 16 - 1) * 16 + entry always names a leaf; slot 0 of row l is l itself; the leaves of a row are distinct. `near_count`: some leaf of every device uses all slots. `far_leaf`: entries name leaves of the row's own top cluster, never the row's leaf; distinct within a row. `far_leaf_count`: some leaf of every device uses all slots. `far_mid`: distinct within a row, never the row's own cluster. `far_top`: distinct within a row, never the row's own cluster.
All inputs are finite; a program needn't handle non-finite values.
Results may differ from a plain program's by a relative error of at most 0.0003.
Values sent between devices are 32-bit elements; how exact they have to be, the bound alone decides.
A program may use at most 64 MiB of HBM per device.

v0:
```python
import jax
import jax.numpy as jnp
from jax import lax
from jax.sharding import PartitionSpec as P

ROOT_THREE = 1.7320508075688772
LENGTH_SCALE = 2.0


def with_halo(shard, sides, width):
    for axis, dim in sides:
        count, length = (lax.axis_size(axis), shard.shape[dim])
        up = [(i, (i + 1) % count) for i in range(count - 1)]
        down = [(j, i) for i, j in up]
        last = lax.slice_in_dim(shard, length - width, length, axis=dim)
        initial = lax.slice_in_dim(shard, 0, width, axis=dim)
        before = lax.ppermute(last, axis, up)
        after = lax.ppermute(initial, axis, down)
        shard = jnp.concatenate([before, shard, after], axis=dim)
    return shard


def matern(targets, sources):
    squared = (targets[0][..., :, None] - sources[0][..., None, :]) ** 2
    squared = squared + (targets[1][..., :, None] - sources[1][..., None, :]) ** 2
    squared = squared + (targets[2][..., :, None] - sources[2][..., None, :]) ** 2
    scaled = jnp.sqrt(squared) * (ROOT_THREE / LENGTH_SCALE)
    return (1.0 + scaled) * jnp.exp(-scaled)


def product(form, left, right):
    return jnp.einsum(form, left, right, precision=lax.Precision.HIGHEST)


def shards(
    points,
    rhs,
    start,
    leaf_skel,
    mid_skel,
    top_skel,
    leaf_basis,
    leaf_transfer,
    mid_transfer,
    noise,
    near,
    near_count,
    far_leaf,
    far_leaf_count,
    far_mid,
    far_top,
):
    per_dev = leaf_basis.shape[0]
    rank = leaf_basis.shape[1]
    leaf_width = leaf_basis.shape[2]
    columns = per_dev * leaf_width
    rhs_rows = rhs.shape[0]
    group_size = lax.axis_size("leaf")
    group_index = lax.axis_index("grp")
    window_points = with_halo(points, ((("grp", "leaf"), 1),), columns).reshape(
        3, 3 * per_dev, leaf_width
    )
    target_points = points.reshape(3, per_dev, leaf_width)
    own_leaf_skel = leaf_skel.reshape(3, per_dev, rank)
    group_skel = lax.all_gather(leaf_skel, "leaf", axis=1, tiled=True).reshape(3, -1, rank)
    all_mid_skel = lax.all_gather(mid_skel, ("grp", "leaf"), axis=1, tiled=True).reshape(
        3, -1, rank
    )
    own_mid_skel = mid_skel.reshape(3, 1, rank)
    all_top_skel = top_skel.reshape(3, -1, rank)
    own_top_skel = lax.dynamic_slice_in_dim(all_top_skel, group_index, 1, 1)

    def operator(values):
        window_values = with_halo(values, ((("grp", "leaf"), 1),), columns).reshape(
            rhs_rows, 3 * per_dev, leaf_width
        )

        def add_near(slot_id, total):
            sources = near[:, slot_id]
            tiles = matern(target_points, window_points[:, sources])
            live = (slot_id < near_count).astype(jnp.float32)
            return total + live[None, :, None] * product(
                "lpq,rlq->rlp", tiles, window_values[:, sources]
            )

        near_part = lax.fori_loop(
            0, near.shape[1], add_near, jnp.zeros((rhs_rows, per_dev, leaf_width), jnp.float32)
        )
        blocks = values.reshape(rhs_rows, per_dev, leaf_width)
        leaf_coef = product("lkp,rlp->lrk", leaf_basis, blocks)
        mid_coef = product("lij,lrj->ri", leaf_transfer, leaf_coef)
        group_coef = lax.all_gather(leaf_coef, "leaf", axis=0, tiled=True)

        def add_far(slot_id, total):
            sources = far_leaf[:, slot_id]
            tiles = matern(own_leaf_skel, group_skel[:, sources])
            live = (slot_id < far_leaf_count).astype(jnp.float32)
            return total + live[:, None, None] * product("lij,lrj->lri", tiles, group_coef[sources])

        leaf_far = lax.fori_loop(
            0, far_leaf.shape[1], add_far, jnp.zeros((per_dev, rhs_rows, rank), jnp.float32)
        )
        all_mid = lax.all_gather(mid_coef[None], ("grp", "leaf"), axis=0, tiled=True)
        mid_sources = far_mid[0]
        mid_tiles = matern(own_mid_skel, all_mid_skel[:, mid_sources])
        mid_far = product("fij,frj->ri", mid_tiles, all_mid[mid_sources])
        partial_top = product("ij,rj->ri", mid_transfer[0], mid_coef)
        top_mine = lax.psum(partial_top, "leaf")
        all_top = lax.all_gather(top_mine[None], "grp", axis=0, tiled=True)
        top_sources = far_top[0]
        top_tiles = matern(own_top_skel, all_top_skel[:, top_sources])
        top_far = product("fij,frj->ri", top_tiles, all_top[top_sources])
        mid_local = mid_far + product("ji,rj->ri", mid_transfer[0], top_far)
        leaf_local = leaf_far + product("lji,rj->lri", leaf_transfer, mid_local)
        far_part = product("lkp,lrk->rlp", leaf_basis, leaf_local).reshape(rhs_rows, columns)
        return noise[0] * values + near_part.reshape(rhs_rows, columns) + far_part

    first_residual = rhs - operator(start)
    image = operator(first_residual)
    sums = lax.psum(
        (jnp.sum(first_residual * image, axis=1), jnp.sum(image * image, axis=1)), ("grp", "leaf")
    )
    total_points = columns * lax.axis_size("grp") * group_size
    alpha = sums[0] / total_points / (sums[1] / total_points + 1e-06)
    updated = start + alpha[:, None] * first_residual
    residual = first_residual - alpha[:, None] * image
    return (updated, residual)


def solution(mesh):
    return jax.shard_map(
        shards,
        mesh=mesh,
        in_specs=(
            P(None, ("grp", "leaf")),
            P(None, ("grp", "leaf")),
            P(None, ("grp", "leaf")),
            P(None, ("grp", "leaf")),
            P(None, ("grp", "leaf")),
            P(),
            P(("grp", "leaf"), None, None),
            P(("grp", "leaf"), None, None),
            P(("grp", "leaf"), None, None),
            P(),
            P(("grp", "leaf"), None),
            P(("grp", "leaf")),
            P(("grp", "leaf"), None),
            P(("grp", "leaf")),
            P(("grp", "leaf"), None),
            P("grp", None),
        ),
        out_specs=(P(None, ("grp", "leaf")), P(None, ("grp", "leaf"))),
        check_vma=False,
    )
```

profile of v0, /device:TPU:1, one launch (start us, length us, event | category | flops | bytes accessed | tf_op | source)
XLA Modules:
  0.0 1023.3 jit_solution(9577001933744166820)
XLA Ops:
  4.7 7.2 collective-permute-start.3
  20.9 16.9 %all_gather.25 = f32[3,16384]{1,0:T(4,128)S(1)} all-gather(f32[3,1024]{1,0:T(4,128)} %param.27), channel_id=1, replica_groups=mesh['grp'=8,'leaf'=16] {'leaf'}, dimensions={1}, use_global_device_ids=true | all-gather | bytes 208896 | tf_op jit(solution)/shard_map/all_gather | solution.py:65
  43.7 19.5 %all_gather.24 = f32[256,8,64]{2,1,0:T(8,128)S(1)} all-gather(f32[16,8,64]{2,1,0:T(8,128)S(1)} %fusion.183), channel_id=1, replica_groups=mesh['grp'=8,'leaf'=16] {'leaf'}, dimensions={0}, use_global_device_ids=true | all-gather | bytes 557056 | tf_op jit(solution)/shard_map/all_gather | solution.py:92
  63.7 63.5 %all-gather = f32[1024,64]{1,0:T(8,128)} all-gather(f32[8,64]{1,0:T(8,128)S(1)} %convolution_bitcast_fusion.9), channel_id=2, replica_groups=mesh['grp'=8,'leaf'=16] {'grp','leaf'}, dimensions={0}, use_global_device_ids=true | all-gather | bytes 264192 | tf_op jit(solution)/shard_map/all_gather | solution.py:103
  127.4 31.0 %psum.28 = f32[1,8,64]{2,1,0:T(8,128)S(1)} all-reduce(f32[1,8,64]{2,1,0:T(8,128)S(1)} %convolution_bitcast_fusion.5), channel_id=1, replica_groups=mesh['grp'=8,'leaf'=16] {'leaf'}, use_global_device_ids=true, to_apply=%region_4.0 | all-reduce | flops 512 | bytes 4096 | tf_op jit(solution)/shard_map/psum | solution.py:108
  158.3 19.8 %all_gather.28 = f32[8,8,64]{2,1,0:T(8,128)S(1)} all-gather(f32[1,8,64]{2,1,0:T(8,128)S(1)} %psum.28), channel_id=1, replica_groups=mesh['grp'=8,'leaf'=16] {'grp'}, dimensions={0}, use_global_device_ids=true | all-gather | bytes 18432 | tf_op jit(solution)/shard_map/all_gather | solution.py:109
  179.9 56.1 %all-gather.2 = f32[128,64,3]{1,2,0:T(4,128)S(1)} all-gather(f32[1,64,3]{1,2,0:T(4,128)S(1)} %bitcast.275), channel_id=1, replica_groups=mesh['grp'=8,'leaf'=16] {'grp','leaf'}, dimensions={0}, use_global_device_ids=true | all-gather | bytes 99072 | tf_op jit(solution)/shard_map/all_gather | solution.py:66
  240.1 142.6 %while.57 = (s32[]{:T(128)}, f32[16,8,64]{2,1,0:T(8,128)S(1)}, s32[16]{0:T(128)}, s32[16,32]{0,1:T(8,128)S(1)}, f32[256,8,64]{2,1,0:T(8,128)S(1)}, /*index=5*/f3...) while((s32[]{:T(128)}, f32[16,8,64]{2,1,0:T(8,128)S(1)}, s32[16]{0:T(128)}, ...), condition=%wide.region_3.0_spmd.clone, body=%wide.region_2.0_spmd.clone.sunk | while | flops 7103571 | bytes 266863 | solution.py:100
  388.8 141.4 %while.56 = (s32[]{:T(128)}, f32[8,16,256]{2,0,1:T(8,128)S(1)}, s32[16]{0:T(128)S(1)}, s32[16,16]{0,1:T(8,128)S(1)}, f32[8,48,256]{2,0,1:T(8,128)S(1)}, /*index=...) while((s32[]{:T(128)}, f32[8,16,256]{2,0,1:T(8,128)S(1)}, ...), condition=%wide.region_1.0_spmd.clone, body=%wide.region_0.0_spmd.clone.sunk | while | flops 113345616 | bytes 1151599 | solution.py:86
  390.1 7.5 fusion.237
  398.9 7.5 fusion.237
  407.7 7.5 fusion.237
  416.6 7.5 fusion.237
  425.4 7.5 fusion.237
  434.2 7.5 fusion.237
  443.1 7.5 fusion.237
  451.9 7.5 fusion.237
  460.8 7.5 fusion.237
  469.6 7.5 fusion.237
  478.4 7.5 fusion.237
  487.3 7.5 fusion.237
  496.1 7.5 fusion.237
  504.9 7.5 fusion.237
  513.8 7.5 fusion.237
  522.6 7.5 fusion.237
  540.8 55.0 %all-gather.1 = f32[1024,64]{1,0:T(8,128)} all-gather(f32[8,64]{1,0:T(8,128)S(1)} %convolution_bitcast_fusion.7), channel_id=3, replica_groups=mesh['grp'=8,'leaf'=16] {'grp','leaf'}, dimensions={0}, use_global_device_ids=true | all-gather | bytes 264192 | tf_op jit(solution)/shard_map/all_gather | solution.py:103
  595.8 18.5 %all_gather.29 = f32[256,8,64]{2,1,0:T(8,128)S(1)} all-gather(f32[16,8,64]{2,1,0:T(8,128)S(1)} %fusion.185), channel_id=1, replica_groups=mesh['grp'=8,'leaf'=16] {'leaf'}, dimensions={0}, use_global_device_ids=true | all-gather | bytes 557056 | tf_op jit(solution)/shard_map/all_gather | solution.py:92
  614.3 30.9 %psum.29 = f32[1,8,64]{2,1,0:T(8,128)S(1)} all-reduce(f32[1,8,64]{2,1,0:T(8,128)S(1)} %convolution_bitcast_fusion.3), channel_id=1, replica_groups=mesh['grp'=8,'leaf'=16] {'leaf'}, use_global_device_ids=true, to_apply=%region_9.0 | all-reduce | flops 512 | bytes 4096 | tf_op jit(solution)/shard_map/psum | solution.py:108
  645.2 25.0 %all_gather.31 = f32[8,8,64]{2,1,0:T(8,128)S(1)} all-gather(f32[1,8,64]{2,1,0:T(8,128)S(1)} %psum.29), channel_id=1, replica_groups=mesh['grp'=8,'leaf'=16] {'grp'}, dimensions={0}, use_global_device_ids=true | all-gather | bytes 18432 | tf_op jit(solution)/shard_map/all_gather | solution.py:109
  674.5 142.6 %while.59 = (s32[]{:T(128)}, f32[16,8,64]{2,1,0:T(8,128)S(1)}, s32[16]{0:T(128)}, s32[16,32]{0,1:T(8,128)S(1)}, f32[256,8,64]{2,1,0:T(8,128)S(1)}, /*index=5*/f3...) while((s32[]{:T(128)}, f32[16,8,64]{2,1,0:T(8,128)S(1)}, s32[16]{0:T(128)}, ...), condition=%wide.region_8.0_spmd.clone, body=%wide.region_7.0_spmd.clone.sunk | while | flops 7103571 | bytes 266863 | solution.py:100
  819.3 141.3 %while.58 = (s32[]{:T(128)}, f32[8,16,256]{2,0,1:T(8,128)S(1)}, s32[16]{0:T(128)S(1)}, s32[16,16]{0,1:T(8,128)S(1)}, f32[8,48,256]{2,0,1:T(8,128)S(1)}, /*index=...) while((s32[]{:T(128)}, f32[8,16,256]{2,0,1:T(8,128)S(1)}, ...), condition=%wide.region_6.0_spmd.clone, body=%wide.region_5.0_spmd.clone.sunk | while | flops 113345616 | bytes 1151599 | solution.py:86
  820.6 7.5 fusion.247
  829.4 7.5 fusion.247
  838.3 7.5 fusion.247
  847.1 7.5 fusion.247
  855.9 7.5 fusion.247
  864.7 7.5 fusion.247
  873.6 7.5 fusion.247
  882.4 7.5 fusion.247
  891.2 7.5 fusion.247
  900.1 7.5 fusion.247
  908.9 7.5 fusion.247
  917.7 7.5 fusion.247
  926.5 7.5 fusion.247
  935.4 7.5 fusion.247
  944.2 7.5 fusion.247
  953.0 7.5 fusion.247
  960.7 61.8 %all-reduce = (f32[8]{0:T(128)S(1)}, f32[8]{0:T(128)S(1)}) all-reduce(f32[8]{0:T(128)S(1)} %get-tuple-element.711, f32[8]{0:T(128)S(1)} %get-tuple-element.710), channel_id=1, replica_groups=mesh['grp'=8,'leaf'=16] {'grp','leaf'}, use_global_device_ids=true, to_apply=%region_13.0 | all-reduce | flops 16 | bytes 128 | tf_op jit(solution)/shard_map/psum | solution.py:120
  (890 shorter events, 369.7 us)
Async XLA Ops:
  0.6 41.1 %copy-start = (f32[16,64,256]{2,1,0:T(8,128)S(1)}, f32[16,64,256]{2,1,0:T(8,128)}, u32[]{:S(2)}) copy-start(f32[16,64,256]{2,1,0:T(8,128)} %param.30) | copy-start | bytes 3145732
  0.6 386.1 %collective-permute-start.2 = (f32[3,4096]{1,0:T(4,128)}, f32[3,4096]{1,0:T(4,128)}, u32[]{:S(2)}, u32[]{:S(2)}) collective-permute-start(f32[3,4096]{1,0:T(4,128)} %param.24), channel_id=1, source_target_pairs={{0,1},{1,2},{2,3},{3,4},{4,5},{5,6},{6,7},{7,8},{8,9},{9,10},{10,1... | collective-permute-start | bytes 147464 | tf_op jit(solution)/shard_map/ppermute | solution.py:17
  4.7 382.0 %collective-permute-start.3 = (f32[3,4096]{1,0:T(4,128)}, f32[3,4096]{1,0:T(4,128)}, u32[]{:S(2)}, u32[]{:S(2)}) collective-permute-start(f32[3,4096]{1,0:T(4,128)} %param.24), channel_id=1, source_target_pairs={{1,0},{2,1},{3,2},{4,3},{5,4},{6,5},{7,6},{8,7},{9,8},{10,9},{11,1... | collective-permute-start | bytes 147464 | tf_op jit(solution)/shard_map/ppermute | solution.py:18
  12.0 375.7 %collective-permute-start = (f32[8,4096]{1,0:T(8,128)}, f32[8,4096]{1,0:T(8,128)}, u32[]{:S(2)}, u32[]{:S(2)}) collective-permute-start(f32[8,4096]{1,0:T(8,128)} %param.26), channel_id=1, source_target_pairs={{0,1},{1,2},{2,3},{3,4},{4,5},{5,6},{6,7},{7,8},{8,9},{9,10},{10,1... | collective-permute-start | bytes 393224 | tf_op jit(solution)/shard_map/ppermute | solution.py:17
  13.9 373.8 %collective-permute-start.1 = (f32[8,4096]{1,0:T(8,128)}, f32[8,4096]{1,0:T(8,128)}, u32[]{:S(2)}, u32[]{:S(2)}) collective-permute-start(f32[8,4096]{1,0:T(8,128)} %param.26), channel_id=1, source_target_pairs={{1,0},{2,1},{3,2},{4,3},{5,4},{6,5},{7,6},{8,7},{9,8},{10,9},{11,1... | collective-permute-start | bytes 393224 | tf_op jit(solution)/shard_map/ppermute | solution.py:18
  39.2 138.9 %copy-start.17 = (s32[1024]{0:T(1024)}, s32[1024]{0:T(1024)S(1)}, u32[]{:S(2)}) copy-start(s32[1024]{0:T(1024)S(1)} %pad_clamp_fusion.4) | copy-start | bytes 12292
  40.0 1.8 copy-start.8
  41.8 21.4 %copy-start.1 = (f32[16,64,64]{2,1,0:T(8,128)S(1)}, f32[16,64,64]{2,1,0:T(8,128)}, u32[]{:S(2)}) copy-start(f32[16,64,64]{2,1,0:T(8,128)} %param.31) | copy-start | bytes 786436
  43.7 83.5 %copy-start.3 = (f32[1,64,64]{2,1,0:T(8,128)S(1)}, f32[1,64,64]{2,1,0:T(8,128)}, u32[]{:S(2)}) copy-start(f32[1,64,64]{2,1,0:T(8,128)} %param.32) | copy-start | bytes 49156
  43.7 135.6 %copy-start.25 = (s32[1,16]{1,0:T(1,128)S(1)}, s32[1,16]{1,0:T(1,128)}, u32[]{:S(2)}) copy-start(s32[1,16]{1,0:T(1,128)} %param.38) | copy-start | bytes 196
  43.7 135.6 %copy-start.18 = (f32[3,64]{1,0:T(4,128)S(1)}, f32[3,64]{1,0:T(4,128)}, u32[]{:S(2)}) copy-start(f32[3,64]{1,0:T(4,128)} %param.28) | copy-start | bytes 2308
  179.3 59.6 %copy-start.16 = (s32[1024]{0:T(1024)}, s32[1024]{0:T(1024)S(1)}, u32[]{:S(2)}) copy-start(s32[1024]{0:T(1024)S(1)} %pad_clamp_fusion.5) | copy-start | bytes 12292
  236.3 3.7 copy-start.10
  236.5 3.6 copy-start.7
  237.1 146.7 %copy-start.12 = (f32[1,16,64]{2,0,1:T(1,128)}, f32[1,16,64]{2,0,1:T(1,128)S(1)}, u32[]{:S(2)}) copy-start(f32[1,16,64]{2,0,1:T(1,128)S(1)} %get-tuple-element.804) | copy-start | bytes 12292
  237.1 146.7 %copy-start.14 = (f32[1,16,64]{2,0,1:T(1,128)}, f32[1,16,64]{2,0,1:T(1,128)S(1)}, u32[]{:S(2)}) copy-start(f32[1,16,64]{2,0,1:T(1,128)S(1)} %get-tuple-element.805) | copy-start | bytes 12292
  240.1 142.7 %copy-start.19 = (f32[1,3,64]{2,0,1:T(1,128)S(1)}, f32[1,3,64]{2,0,1:T(1,128)}, u32[]{:S(2)}) copy-start(f32[1,3,64]{2,0,1:T(1,128)} %get-tuple-element.810) | copy-start | bytes 2308
  240.1 142.7 %copy-start.20 = (f32[1,3,64]{2,0,1:T(1,128)S(1)}, f32[1,3,64]{2,0,1:T(1,128)}, u32[]{:S(2)}) copy-start(f32[1,3,64]{2,0,1:T(1,128)} %get-tuple-element.811) | copy-start | bytes 2308
  240.1 143.4 %copy-start.9 = (f32[3,8,64]{2,1,0:T(8,128)S(1)}, f32[3,8,64]{2,1,0:T(8,128)}, u32[]{:S(2)}) copy-start(f32[3,8,64]{2,1,0:T(8,128)} %gather_fusion.10) | copy-start | bytes 18436
  240.1 143.4 %copy-start.21 = (f32[1,3,64]{2,1,0:T(4,128)S(1)}, f32[1,3,64]{2,1,0:T(4,128)}, u32[]{:S(2)}) copy-start(f32[1,3,64]{2,1,0:T(4,128)} %copy.71) | copy-start | bytes 2308
  240.1 143.8 %copy-start.22 = (f32[64]{0:T(128)S(1)}, f32[64]{0:T(128)}, u32[]{:S(2)}) copy-start(f32[64]{0:T(128)} %get-tuple-element.812) | copy-start | bytes 772
  240.1 143.8 %copy-start.23 = (f32[64]{0:T(128)S(1)}, f32[64]{0:T(128)}, u32[]{:S(2)}) copy-start(f32[64]{0:T(128)} %get-tuple-element.813) | copy-start | bytes 772
  240.1 143.8 %copy-start.24 = (f32[64]{0:T(128)S(1)}, f32[64]{0:T(128)}, u32[]{:S(2)}) copy-start(f32[64]{0:T(128)} %get-tuple-element.814) | copy-start | bytes 772
  384.8 1.2 copy-start.5
  384.8 1.2 copy-start.11
  385.3 2.4 copy-start.2
  385.3 3.4 copy-start.26
  388.7 141.4 %copy-start.6 = (f32[8,4096]{1,0:T(8,128)S(1)}, f32[8,4096]{1,0:T(8,128)}, u32[]{:S(2)}) copy-start(f32[8,4096]{1,0:T(8,128)} %param.25) | copy-start | bytes 393220
  530.2 10.4 %copy-start.4 = (f32[1,64,64]{2,1,0:T(8,128)S(1)}, f32[1,64,64]{2,1,0:T(8,128)}, u32[]{:S(2)}) copy-start(f32[1,64,64]{2,1,0:T(8,128)} %param.32) | copy-start | bytes 49156
  530.2 288.0 %collective-permute-start.4 = (f32[8,4096]{1,0:T(8,128)S(1)}, f32[8,4096]{1,0:T(8,128)}, u32[]{:S(2)}, u32[]{:S(2)}) collective-permute-start(f32[8,4096]{1,0:T(8,128)S(1)} %add_subtract_fusion), channel_id=1, source_target_pairs={{0,1},{1,2},{2,3},{3,4},{4,5},{5,6},{6,7},{7,8},{8,9},{9,10},{10,1... | collective-permute-start | bytes 393224 | tf_op jit(solution)/shard_map/ppermute | solution.py:17
  533.7 284.6 %collective-permute-start.5 = (f32[8,4096]{1,0:T(8,128)S(1)}, f32[8,4096]{1,0:T(8,128)}, u32[]{:S(2)}, u32[]{:S(2)}) collective-permute-start(f32[8,4096]{1,0:T(8,128)S(1)} %add_subtract_fusion), channel_id=1, source_target_pairs={{1,0},{2,1},{3,2},{4,3},{5,4},{6,5},{7,6},{8,7},{9,8},{10,9},{11,1... | collective-permute-start | bytes 393224 | tf_op jit(solution)/shard_map/ppermute | solution.py:18
  540.8 132.1 %copy-start.13 = (f32[1,16,64]{2,0,1:T(1,128)S(1)}, f32[1,16,64]{2,0,1:T(1,128)}, u32[]{:S(2)}) copy-start(f32[1,16,64]{2,0,1:T(1,128)} %copy-done.12) | copy-start | bytes 12292
  540.8 132.1 %copy-start.15 = (f32[1,16,64]{2,0,1:T(1,128)S(1)}, f32[1,16,64]{2,0,1:T(1,128)}, u32[]{:S(2)}) copy-start(f32[1,16,64]{2,0,1:T(1,128)} %copy-done.14) | copy-start | bytes 12292
  817.6 1.6 copy-start.27
where the time goes:
time: 1030 us; the launch traced here: 1020 us
  blocking collectives  398 us (39%)
  matrix products  347 us (34%)
  local copies, waits for them, and re-layouts  193 us (19%)
  other arithmetic  48.7 us (5%)
  starting transfers between devices  29.1 us (3%)
    dot_general x112, matrix products, product(): return jnp.einsum(form, left, right, precision=lax.Precision.HIGHEST)  347 us
    all_gather x2, blocking collectives, operator(): lax.all_gather(mid_coef[None], ('grp', 'leaf'), axis=0, tiled=True)  118 us
    gather x64, local copies, waits for them, and re-layouts, add_far(): tiles = matern(own_leaf_skel, group_skel[:, sources])  104 us
    psum x2, blocking collectives, operator(): top_mine = lax.psum(partial_top, 'leaf')  61.8 us
    psum x1, blocking collectives, shards(): lax.psum((jnp.sum(first_residual * image, axis=1), jnp.sum(image * image,...  61.8 us
    all_gather x1, blocking collectives, shards(): lax.all_gather(mid_skel, ('grp', 'leaf'), axis=1, tiled=True)  56.1 us
    all_gather x2, blocking collectives, operator(): all_top = lax.all_gather(top_mine[None], 'grp', axis=0, tiled=True)  44.8 us
    convert_element_type x64, other arithmetic, add_far(): live = (slot_id < far_leaf_count).astype(jnp.float32)  42.3 us
  transfers between devices with their start and end apart: 6, of which 0 were waited for; matrix products, arithmetic and copies ran while one was open for 30% of the time, Pallas kernels for 0%

commit v1 on v0

v1 whole, which is shorter than its diff:
```python
import functools
import math

import jax
import jax.numpy as jnp
import numpy as np
from jax import lax
from jax.experimental import pallas as pl
from jax.experimental.pallas import tpu as pltpu
from jax.sharding import PartitionSpec as P

BF = jnp.bfloat16
F32 = jnp.float32
MESH = pl.DeviceIdType.MESH
NT = (((1,), (1,)), ((), ()))

LEAF = 256
RANK = 64
RHS = 8
PER = 16
NEAR = 16
FARL = 32
FARM = 16
FART = 3
GROUPS = 8
GSIZE = 16
LEAVES = 2048
WIN = 3 * PER
PIECES = 48
UNROLL = 4

LOG2E = math.log2(math.e)
KAPPA = 0.75 * LOG2E * LOG2E
FACTOR = math.e * math.log(2.0)
TINY = 1e-30


def morton_table():
    ids = np.arange(LEAVES)
    coords = [np.zeros_like(ids) for _ in range(3)]
    for bit in range(30):
        coords[bit % 3] += ((ids >> bit) & 1) << (bit // 3)
    packed = coords[0] + 256 * coords[1] + 65536 * coords[2]
    return np.pad(packed, (PER, PER)).astype(np.int32)


def tangent_tables():
    mean = 0.75 * (np.arange(512) + 0.5)
    s = np.sqrt(mean)
    beta = 0.5 * np.exp(-s) / (LOG2E * LOG2E) / FACTOR
    alpha = -(1 + s) * np.exp(-s) / FACTOR - beta * mean * LOG2E * LOG2E
    return alpha.astype(np.float32), beta.astype(np.float32)


def rounded(x):
    return x.astype(BF).astype(F32)


def split2(x):
    high = rounded(x)
    return jnp.concatenate([high, x - high], axis=0).astype(BF)


def split3(x):
    first = rounded(x)
    rest = x - first
    second = rounded(rest)
    return first, second, rounded(rest - second)


def source_pieces(w):
    a, b, c = split3(w)
    return jnp.concatenate([a, b, a, b, c, a], axis=0)


def target_pieces(u):
    a, b, c = split3(u)
    return jnp.concatenate([a, a, b, b, a, c], axis=0)


def rows_of(shape):
    return lax.broadcasted_iota(jnp.int32, shape, 0)


def source_rows(x):
    row = rows_of(x.shape)
    x = jnp.where(row < 3, x, 0.0)
    norm = KAPPA * jnp.sum(x * x, axis=0, keepdims=True)
    return jnp.where(row == 3, norm, jnp.where(row == 4, 1.0, x))


def target_rows(x):
    row = rows_of(x.shape)
    x = jnp.where(row < 3, x, 0.0)
    norm = KAPPA * jnp.sum(x * x, axis=0, keepdims=True)
    return jnp.where(row == 4, norm, jnp.where(row == 3, 1.0, (-2.0 * KAPPA) * x))


def kernel_value(q):
    q = jnp.maximum(q, TINY)
    y = -LOG2E - q * lax.rsqrt(q)
    return y * jnp.exp2(y)


def halves(x):
    high = x.astype(BF)
    return high, (x - high.astype(F32)).astype(BF)


def dot(a, b):
    return jnp.dot(a, b, preferred_element_type=F32)


def dot_nt(a, b):
    return lax.dot_general(a, b, NT, preferred_element_type=F32)


def fold(x):
    return x[:RHS] + x[RHS:]


def body(
    points,
    rhs,
    start,
    leaf_skel,
    mid_skel,
    top_skel,
    basis,
    transfer,
    mid_transfer,
    noise,
    near,
    near_count,
    far_leaf,
    far_count,
    far_mid,
    far_top,
    corners,
    alphas,
    betas,
    updated,
    residual,
    remainder,
    qa,
    qb,
    far_high,
    far_low,
    mid_high,
    mid_low,
    top_high,
    top_low,
    halo1,
    halo2,
    gather1,
    gather2,
    mids1,
    mids2,
    all1,
    all2,
    sums1,
    sums2,
    field,
    wfeat,
    ufeat,
    wrows,
    urows,
    moments,
    skel_feat,
    mid_feat,
    top_feat,
    top_tiles,
    basis_high,
    basis_low,
    transfer2,
    near_acc,
    local,
    image,
    first,
    halo_send,
    halo_recv,
    mid_send,
    mid_recv,
    coef_send,
    coef_recv,
    all_send,
    all_recv,
    sum_send,
    sum_recv,
    tot_send,
    tot_recv,
):
    g = lax.axis_index("grp")
    i = lax.axis_index("leaf")
    lane = lax.broadcasted_iota(jnp.int32, (RHS, 128), 1)
    low_lanes = lane < RANK

    def peer_leaf(k):
        return (g, lax.rem(i + k, GSIZE))

    def peer_grp(k):
        return (lax.rem(g + k, GROUPS), i)

    up = i + 1
    down = i + GSIZE - 1
    after = (lax.rem(g + lax.div(up, GSIZE), GROUPS), lax.rem(up, GSIZE))
    before = (lax.rem(g + GROUPS - 1 + lax.div(down, GSIZE), GROUPS), lax.rem(down, GSIZE))

    barrier = pltpu.get_barrier_semaphore()
    partners = (
        [peer_leaf(k) for k in range(1, GSIZE)]
        + [peer_grp(k) for k in range(1, GROUPS)]
        + [after, before]
    )
    for partner in partners:
        pl.semaphore_signal(barrier, inc=1, device_id=partner, device_id_type=MESH)

    def remote(src, dst, send, recv, device):
        return pltpu.make_async_remote_copy(
            src_ref=src,
            dst_ref=dst,
            send_sem=send,
            recv_sem=recv,
            device_id=device,
            device_id_type=MESH,
        )

    def halo_copies(window, phase):
        own = window.at[1]
        return [
            remote(own, window.at[0], halo_send.at[phase, 0], halo_recv.at[phase, 0], after),
            remote(own, window.at[2], halo_send.at[phase, 1], halo_recv.at[phase, 1], before),
        ]

    def leaf_copies(buffer, send, recv, phase):
        return [
            remote(buffer.at[i], buffer.at[i], send.at[phase, k], recv.at[phase, i], peer_leaf(k))
            for k in range(1, GSIZE)
        ]

    def wait_leaf(buffer, send, recv, phase):
        for k in range(1, GSIZE):
            src = lax.rem(i + k, GSIZE)
            remote(
                buffer.at[src], buffer.at[src], send.at[phase, k], recv.at[phase, src], peer_leaf(k)
            ).wait_recv()

    def grp_copies(buffer, send, recv, phase):
        return [
            remote(buffer.at[g], buffer.at[g], send.at[phase, k], recv.at[phase, g], peer_grp(k))
            for k in range(1, GROUPS)
        ]

    def wait_grp(buffer, send, recv, phase):
        for k in range(1, GROUPS):
            src = lax.rem(g + k, GROUPS)
            remote(
                buffer.at[src], buffer.at[src], send.at[phase, k], recv.at[phase, src], peer_grp(k)
            ).wait_recv()

    pending = []

    def launch(copies):
        for copy in copies:
            copy.start()
        pending.extend(copies)

    def coefficients(read, tiles, mid_tile):
        def pair(p, carry):
            parts = []
            for side in range(2):
                leaf = 2 * p + side
                v = split2(read(leaf))
                field[PER + leaf] = v
                both = dot_nt(v, basis_high[leaf]) + dot_nt(v, basis_low[leaf])
                parts.append(fold(both))
            tiles[p] = jnp.concatenate(parts, axis=1)
            return carry

        lax.fori_loop(0, PER // 2, pair, 0)
        total = jnp.zeros((2 * RHS, RANK), F32)
        for p in range(PER // 2):
            c = split2(tiles[p])
            for part in range(2):
                total += dot_nt(c, transfer2[part, :, 128 * p : 128 * (p + 1)])
        mid = fold(total)
        m = split2(mid)
        own = mid_transfer[0]
        high, low = halves(own)
        top = fold(dot_nt(m, high) + dot_nt(m, low))
        mid_tile[...] = jnp.concatenate([mid, top], axis=1)

    for leaf in range(PER):
        high, low = halves(basis[leaf])
        basis_high[leaf] = high
        basis_low[leaf] = low
    for p in range(PER // 2):
        both = jnp.concatenate([transfer[2 * p], transfer[2 * p + 1]], axis=1)
        high, low = halves(both)
        transfer2[0, :, 128 * p : 128 * (p + 1)] = high
        transfer2[1, :, 128 * p : 128 * (p + 1)] = low

    halo1[1, 0] = jnp.zeros((8, PER * LEAF), F32)
    halo1[1, 0, 0:3, :] = points[...]
    halo1[1, 1] = start[...]
    own_gather = gather1.at[i]
    for p in range(PER // 2):
        own_gather[PER // 2 + p] = jnp.zeros((8, 128), F32)
        own_gather[PER // 2 + p, 0:3, :] = leaf_skel[:, 128 * p : 128 * (p + 1)]
    mids1[i, 1] = jnp.zeros((8, 128), F32)
    mids1[i, 1, 0:3, 0:RANK] = mid_skel[...]

    def column(leaf):
        return pl.ds(pl.multiple_of(leaf * LEAF, LEAF), LEAF)

    coefficients(lambda leaf: start[:, column(leaf)], gather1.at[i], mids1.at[i, 0])

    pl.semaphore_wait(barrier, len(partners))
    launch(halo_copies(halo1, 0))
    launch(leaf_copies(mids1, mid_send, mid_recv, 0))
    launch(leaf_copies(gather1, coef_send, coef_recv, 0))

    centre = jnp.floor(halo1[1, 0, :, 0:1])

    def window_features(leaf, block, place):
        x = halo1[block, 0, :, column(place)] - centre
        w = source_rows(x)
        wrows[leaf] = w
        wfeat[leaf] = source_pieces(w).T.astype(BF)
        return x

    def own_features(l, carry):
        x = window_features(PER + l, 1, l)
        u = target_rows(x)
        urows[l] = u
        ufeat[l] = target_pieces(u).astype(BF)
        return carry

    lax.fori_loop(0, PER, own_features, 0)
    for p in range(PER // 2):
        u = target_pieces(target_rows(own_gather[PER // 2 + p] - centre))
        skel_feat[128 * p : 128 * (p + 1), :] = u.T.astype(BF)
    u = target_pieces(target_rows(mids1[i, 1] - centre))
    mid_feat[...] = u.T.astype(BF)
    for p in range(GROUPS // 2):
        top_tiles[p] = jnp.zeros((8, 128), F32)
        top_tiles[p, 0:3, :] = top_skel[:, 128 * p : 128 * (p + 1)]
    tile = top_tiles[lax.div(g, 2)]
    tile = jnp.where(lax.rem(g, 2) == 0, tile, pltpu.roll(tile, RANK, 1))
    top_feat[...] = target_pieces(target_rows(tile - centre)).T.astype(BF)

    def window_moments(leaf, v):
        for k in range(5):
            total = jnp.sum(v * wrows[leaf, k : k + 1, :], axis=1, keepdims=True)
            moments[leaf, k] = jnp.broadcast_to(total, (RHS, 128))

    def own_moments(read):
        def one(l, carry):
            window_moments(PER + l, read(l))
            return carry

        lax.fori_loop(0, PER, one, 0)

    own_moments(lambda l: start[:, column(l)])
    for copy in halo_copies(halo1, 0):
        copy.wait_recv()

    def edge_features(l, carry):
        for block in (0, 2):
            leaf = block * PER + l
            window_features(leaf, block, l)
            v = halo1[block, 1, :, column(l)]
            field[leaf] = split2(v)
            window_moments(leaf, v)
        return carry

    lax.fori_loop(0, PER, edge_features, 0)

    wait_leaf(mids1, mid_send, mid_recv, 0)
    all1[g] = mids1[...]
    launch(grp_copies(all1, all_send, all_recv, 0))

    device = g * GSIZE + i
    base = device * PER

    def distance2(l, s):
        a = corners[base + PER + l]
        b = corners[base + near[l, s]]
        dx = (a & 255) - (b & 255)
        dy = ((a >> 8) & 255) - ((b >> 8) & 255)
        dz = (a >> 16) - (b >> 16)
        return jnp.minimum(dx * dx + dy * dy + dz * dz, 511)

    def fill(ref, l, s0):
        for t in range(UNROLL):
            ref[t] = dot(wfeat[near[l, s0 + t]], ufeat[l])

    def evaluate(ref, l, s0):
        for t in range(UNROLL):
            d2 = distance2(l, s0 + t)
            alpha, beta = alphas[d2], betas[d2]
            for c in range(0, LEAF, 64):
                q = ref[t, c : c + 64, :]
                r = kernel_value(q) - (q * beta + alpha)
                remainder[l * NEAR + s0 + t, c : c + 64, :] = r.astype(BF)

    def multiply(l, s0, count):
        total = jnp.zeros((2 * RHS, LEAF), F32)
        for t in range(count):
            s = s0 + t
            v = field[near[l, s]]
            v = jnp.where(s < near_count[l], v, jnp.zeros_like(v))
            total += dot(v, remainder[l * NEAR + s])
        return total

    def tangent_part(l):
        sums = [jnp.zeros((RHS, 128), F32) for _ in range(5)]
        for s in range(NEAR):
            d2 = distance2(l, s)
            live = jnp.where(s < near_count[l], 1.0, 0.0)
            alpha, beta = alphas[d2] * live, betas[d2] * live
            j = near[l, s]
            for k in range(5):
                sums[k] += beta * moments[j, k]
            sums[3] += alpha * moments[j, 4]
        total = jnp.zeros((RHS, LEAF), F32)
        for k in range(5):
            c = jnp.concatenate([sums[k], sums[k]], axis=1)
            total += c * urows[l, k : k + 1, :]
        return total

    steps = PER * NEAR // UNROLL
    per_leaf = NEAR // UNROLL

    def place(step):
        return lax.div(step, per_leaf), lax.rem(step, per_leaf) * UNROLL

    near_acc[...] = jnp.zeros((PER, 2 * RHS, LEAF), F32)
    fill(qa, 0, 0)

    def near_step(n, carry):
        step = 2 * n
        l0, s0 = place(step)
        l1, s1 = place(step + 1)
        l2, s2 = place(jnp.minimum(step + 2, steps - 1))
        lp, sp = place(jnp.maximum(step - 1, 0))
        fill(qb, l1, s1)
        evaluate(qa, l0, s0)
        fill(qa, l2, s2)
        near_acc[l0] += multiply(l0, s0, UNROLL)
        evaluate(qb, l1, s1)
        near_acc[l1] += multiply(l1, s1, UNROLL)
        return carry

    lax.fori_loop(0, steps // 2, near_step, 0)

    def picked(read, index, want):
        tile = read(index)
        return jnp.where(lax.rem(index, 2) == want, tile, pltpu.roll(tile, RANK, 1))

    def joined(first_tile, second_tile):
        return jnp.where(low_lanes, first_tile, second_tile)

    def far_tiles(feat, tile):
        w = source_pieces(source_rows(tile - centre)).astype(BF)
        return halves(kernel_value(dot(feat, w)))

    def leaf_tile(buffer, offset):
        def read(j):
            return buffer[lax.div(j, GSIZE), offset + lax.div(lax.rem(j, GSIZE), 2)]

        return read

    def far_matrix(lp, carry):
        read = leaf_tile(gather1, PER // 2)
        for side in range(2):
            l = 2 * lp + side
            feat = skel_feat[pl.ds(pl.multiple_of(l * RANK, RANK), RANK), :]
            for p in range(FARL // 2):
                tile = joined(
                    picked(read, far_leaf[l, 2 * p], 0), picked(read, far_leaf[l, 2 * p + 1], 1)
                )
                high, low = far_tiles(feat, tile)
                far_high[l, :, 128 * p : 128 * (p + 1)] = high
                far_low[l, :, 128 * p : 128 * (p + 1)] = low
        return carry

    def far_leaves(buffer):
        read = leaf_tile(buffer, 0)

        def pair(lp, carry):
            parts = []
            for side in range(2):
                l = 2 * lp + side
                cols = []
                for p in range(FARL // 2):
                    s = 2 * p
                    tile = joined(
                        picked(read, far_leaf[l, s], 0), picked(read, far_leaf[l, s + 1], 1)
                    )
                    count = far_count[l]
                    slot = s + jnp.where(low_lanes, 0, 1)
                    cols.append(split2(jnp.where(slot < count, tile, 0.0)))
                c = jnp.concatenate(cols, axis=1)
                parts.append(fold(dot_nt(c, far_high[l]) + dot_nt(c, far_low[l])))
            local[lp] = -FACTOR * jnp.concatenate(parts, axis=1)
            return carry

        lax.fori_loop(0, PER // 2, pair, 0)

    def upper_matrix(buffer):
        def read_mid(m):
            return buffer[lax.div(m, GSIZE), lax.rem(m, GSIZE), 1]

        for p in range(FARM // 2):
            one, two = read_mid(far_mid[0, 2 * p]), read_mid(far_mid[0, 2 * p + 1])
            high, low = far_tiles(
                mid_feat[0:RANK, :], joined(one, pltpu.roll(two, RANK, 1))
            )
            mid_high[:, 128 * p : 128 * (p + 1)] = high
            mid_low[:, 128 * p : 128 * (p + 1)] = low

        def read_top(j):
            return top_tiles[lax.div(j, 2)]

        for p in range(2):
            j1 = far_top[0, 2 * p]
            j2 = far_top[0, min(2 * p + 1, FART - 1)]
            high, low = far_tiles(
                top_feat[0:RANK, :], joined(picked(read_top, j1, 0), picked(read_top, j2, 1))
            )
            top_high[:, 128 * p : 128 * (p + 1)] = high
            top_low[:, 128 * p : 128 * (p + 1)] = low

    def upper_local(read):
        cols = []
        for p in range(FARM // 2):
            one, two = read(far_mid[0, 2 * p]), read(far_mid[0, 2 * p + 1])
            cols.append(split2(joined(one, pltpu.roll(two, RANK, 1))))
        c = jnp.concatenate(cols, axis=1)
        mid_far = -FACTOR * fold(dot_nt(c, mid_high[...]) + dot_nt(c, mid_low[...]))

        def top(j):
            total = jnp.zeros((RHS, 128), F32)
            for m in range(GSIZE):
                total += read(j * GSIZE + m)
            return total

        t0, t1, t2 = (top(far_top[0, s]) for s in range(FART))
        cols = [
            split2(joined(pltpu.roll(t0, RANK, 1), t1)),
            split2(joined(pltpu.roll(t2, RANK, 1), jnp.zeros((RHS, 128), F32))),
        ]
        c = jnp.concatenate(cols, axis=1)
        top_far = -FACTOR * fold(dot_nt(c, top_high[...]) + dot_nt(c, top_low[...]))
        high, low = halves(mid_transfer[0])
        t = split2(top_far)
        return mid_far + fold(dot(t, high) + dot(t, low))

    def finish(read_mid, store):
        m = split2(upper_local(read_mid))
        for p in range(PER // 2):
            down_part = sum(dot(m, transfer2[part, :, 128 * p : 128 * (p + 1)]) for part in range(2))
            local[p] += fold(down_part)

        def pair(lp, carry):
            tile = local[lp]
            for side in range(2):
                l = 2 * lp + side
                c = split2(tile[:, RANK * side : RANK * (side + 1)])
                far = fold(dot(c, basis_high[l]) + dot(c, basis_low[l]))
                near_part = -FACTOR * (fold(near_acc[l]) + tangent_part(l))
                store(l, near_part + far)
            return carry

        lax.fori_loop(0, PER // 2, pair, 0)

    wait_leaf(gather1, coef_send, coef_recv, 0)
    lax.fori_loop(0, PER // 2, far_matrix, 0)
    far_leaves(gather1)
    wait_grp(all1, all_send, all_recv, 0)
    upper_matrix(all1)
    noise_value = noise[0]

    def store_first(l, value):
        cols = column(l)
        r = rhs[:, cols] - (noise_value * start[:, cols] + value)
        first[l] = r
        halo2[1, :, cols] = r

    finish(lambda m: all1[lax.div(m, GSIZE), lax.rem(m, GSIZE), 0], store_first)

    launch(halo_copies(halo2, 1))
    coefficients(lambda leaf: first[leaf], gather2.at[i], mids2.at[i])
    launch(leaf_copies(mids2, mid_send, mid_recv, 1))
    launch(leaf_copies(gather2, coef_send, coef_recv, 1))
    own_moments(lambda l: first[l])
    for copy in halo_copies(halo2, 1):
        copy.wait_recv()

    def edge_moments(l, carry):
        for block in (0, 2):
            leaf = block * PER + l
            v = halo2[block, :, column(l)]
            field[leaf] = split2(v)
            window_moments(leaf, v)
        return carry

    lax.fori_loop(0, PER, edge_moments, 0)
    wait_leaf(mids2, mid_send, mid_recv, 1)
    all2[g] = mids2[...]
    launch(grp_copies(all2, all_send, all_recv, 1))

    def near_again(l, carry):
        near_acc[l] = multiply(l, 0, NEAR)
        return carry

    lax.fori_loop(0, PER, near_again, 0)
    wait_leaf(gather2, coef_send, coef_recv, 1)
    far_leaves(gather2)
    wait_grp(all2, all_send, all_recv, 1)

    def store_image(l, value):
        image[l] = noise_value * first[l] + value

    finish(lambda m: all2[lax.div(m, GSIZE), lax.rem(m, GSIZE)], store_image)

    dots = jnp.zeros((RHS, LEAF), F32)
    squares = jnp.zeros((RHS, LEAF), F32)
    for l in range(PER):
        dots += first[l] * image[l]
        squares += image[l] * image[l]
    sums1[i] = jnp.where(
        low_lanes,
        jnp.sum(dots, axis=1, keepdims=True),
        jnp.sum(squares, axis=1, keepdims=True),
    )
    launch(leaf_copies(sums1, sum_send, sum_recv, 0))
    wait_leaf(sums1, sum_send, sum_recv, 0)
    total = sums1[0]
    for k in range(1, GSIZE):
        total += sums1[k]
    sums2[g] = total
    launch(grp_copies(sums2, tot_send, tot_recv, 0))
    wait_grp(sums2, tot_send, tot_recv, 0)
    total = sums2[0]
    for k in range(1, GROUPS):
        total += sums2[k]
    total = total / (LEAVES * LEAF)
    alpha = total[:, 0:1] / (total[:, RANK : RANK + 1] + 1e-6)
    for l in range(PER):
        cols = slice(l * LEAF, (l + 1) * LEAF)
        r = first[l]
        updated[:, cols] = start[:, cols] + alpha * r
        residual[:, cols] = r - alpha * image[l]
    for copy in pending:
        copy.wait_send()


def shards(*args):
    smem = pl.BlockSpec(memory_space=pltpu.SMEM)
    vmem = pl.BlockSpec(memory_space=pltpu.VMEM)
    alphas, betas = tangent_tables()
    tables = (jnp.asarray(morton_table()), jnp.asarray(alphas), jnp.asarray(betas))
    out = jax.ShapeDtypeStruct((RHS, PER * LEAF), F32)
    tile = (8, 128)

    def buffer(shape, dtype=F32):
        return pltpu.VMEM(shape, dtype)

    def sems(*shape):
        return pltpu.SemaphoreType.DMA(shape)

    scratch = [
        buffer((PER * NEAR, LEAF, LEAF), BF),
        buffer((UNROLL, LEAF, LEAF)),
        buffer((UNROLL, LEAF, LEAF)),
        buffer((PER, RANK, FARL * RANK), BF),
        buffer((PER, RANK, FARL * RANK), BF),
        buffer((RANK, FARM * RANK), BF),
        buffer((RANK, FARM * RANK), BF),
        buffer((RANK, 4 * RANK), BF),
        buffer((RANK, 4 * RANK), BF),
        buffer((3, 2, 8, PER * LEAF)),
        buffer((3, 8, PER * LEAF)),
        buffer((GSIZE, PER) + tile),
        buffer((GSIZE, PER // 2) + tile),
        buffer((GSIZE, 2) + tile),
        buffer((GSIZE,) + tile),
        buffer((GROUPS, GSIZE, 2) + tile),
        buffer((GROUPS, GSIZE) + tile),
        buffer((GSIZE,) + tile),
        buffer((GROUPS,) + tile),
        buffer((WIN, 2 * RHS, LEAF), BF),
        buffer((WIN, LEAF, PIECES), BF),
        buffer((PER, PIECES, LEAF), BF),
        buffer((WIN, 8, LEAF)),
        buffer((PER, 8, LEAF)),
        buffer((WIN, 5) + tile),
        buffer((PER * RANK, PIECES), BF),
        buffer((128, PIECES), BF),
        buffer((128, PIECES), BF),
        buffer((GROUPS // 2,) + tile),
        buffer((PER, RANK, LEAF), BF),
        buffer((PER, RANK, LEAF), BF),
        buffer((2, RANK, PER * RANK), BF),
        buffer((PER, 2 * RHS, LEAF)),
        buffer((PER // 2,) + tile),
        buffer((PER, RHS, LEAF)),
        buffer((PER, RHS, LEAF)),
        sems(2, 2),
        sems(2, 2),
        sems(2, GSIZE),
        sems(2, GSIZE),
        sems(2, GSIZE),
        sems(2, GSIZE),
        sems(2, GROUPS),
        sems(2, GROUPS),
        sems(1, GSIZE),
        sems(1, GSIZE),
        sems(1, GROUPS),
        sems(1, GROUPS),
    ]
    return pl.pallas_call(
        body,
        out_shape=(out, out),
        in_specs=[vmem] * 9 + [smem] * 10,
        out_specs=(vmem, vmem),
        scratch_shapes=scratch,
        compiler_params=pltpu.CompilerParams(
            collective_id=0, has_side_effects=True, vmem_limit_bytes=61 << 20
        ),
    )(*args, *tables)


def solution(mesh):
    columns = P(None, ("grp", "leaf"))
    blocks = P(("grp", "leaf"), None, None)
    lists = P(("grp", "leaf"), None)
    return jax.shard_map(
        shards,
        mesh=mesh,
        in_specs=(
            columns,
            columns,
            columns,
            columns,
            columns,
            P(),
            blocks,
            blocks,
            blocks,
            P(),
            lists,
            P(("grp", "leaf")),
            lists,
            P(("grp", "leaf")),
            lists,
            P("grp", None),
        ),
        out_specs=(columns, columns),
        check_vma=False,
    )
```

time: 1030 us -> 121 us (0.12)
  blocking collectives: 398 us -> 0 us
  matrix products: 347 us -> 0 us
  local copies, waits for them, and re-layouts: 193 us -> 2.26 us
  Pallas kernels: 0 us -> 117 us
  other arithmetic: 48.7 us -> 0 us
  starting transfers between devices: 29.1 us -> 0 us
    dot_general x112 -> x0, matrix products: 347 us -> none  [product(): return jnp.einsum(form, left, right, precision=lax.Precision.HIGHEST)]
    all_gather x8 -> x0, blocking collectives: 274 us -> none  [the longest x2 118 us: operator(): lax.all_gather(mid_coef[None], ('grp', 'leaf'), axis=0, tiled=True)]
    gather x198 -> x0, local copies, waits for them, and re-layouts: 184 us -> none  [the longest x64 104 us: add_far(): tiles = matern(own_leaf_skel, group_skel[:, sources])]
    psum x3 -> x0, blocking collectives: 124 us -> none  [the longest x2 61.8 us: operator(): top_mine = lax.psum(partial_top, 'leaf')]
    pallas_call x0 -> x1, Pallas kernels: none -> 117 us  [shards(): pl.pallas_call(body, out_shape=(out, out), in_specs=[vmem] * 9 + [smem] *...]
    convert_element_type x96 -> x0, other arithmetic: 42.4 us -> none  [the longest x64 42.3 us: add_far(): live = (slot_id < far_leaf_count).astype(jnp.float32)]
    ppermute x6 -> x0, starting transfers between devices: 29.1 us -> none  [the longest x3 19.7 us: with_halo(): after = lax.ppermute(initial, axis, down)]
  transfers between devices with their start and end apart: 6 -> 0, of which waited for: 0 -> 0; matrix products, arithmetic and copies ran while one was open for 30% -> 0% of each run, Pallas kernels for 0% -> 0%
where the time goes in v1:
time: 121 us
  Pallas kernels  117 us (97%)
  local copies, waits for them, and re-layouts  2.26 us (2%)
  between operations  1.3 us (1%)
    pallas_call x1, Pallas kernels, shards(): pl.pallas_call(body, out_shape=(out, out), in_specs=[vmem] * 9 + [smem] *...  117 us

profile of v1, /device:TPU:1, one launch (start us, length us, event | category | flops | bytes accessed | tf_op | source)
XLA Modules:
  0.0 120.9 jit_solution(17050738232841179091)
XLA Ops:
  1.3 117.4 %shard_map.194 = (f32[8,4096]{1,0:T(8,128)}, f32[8,4096]{1,0:T(8,128)}) custom-call(f32[3,4096]{1,0:T(4,128)} %points.1, f32[8,4096]{1,0:T(8,128)} %rhs.1, f32[8,4096]{1,0:T(8,128)} %start.1, f32[3,1024]{1,0:T(4,128)} %leaf_skel.1, f32[3,64]{1,0:T(4,128)} %mid_skel.1, f32[3,512]{1,0:T(4,128)} %top_skel.1, f32[16,64,256]{2,1,0:T(8,128)} %basis.1, ...), custom_call_target="tpu_custom_call" | custom-call | tf_op jit(solution)/shard_map/pallas_call | solution.py:724
  118.7 0.0 copy-start
  118.7 1.6 %copy.24 = f32[8,4096]{1,0:T(8,128)} copy(f32[8,4096]{1,0:T(8,128)} %get-tuple-element.4) | data formatting | bytes 262144
  120.3 0.0 copy-done
  120.3 0.7 copy.25
Async XLA Ops:
  118.7 1.6 %copy-start = (f32[8,4096]{1,0:T(8,128)S(1)}, f32[8,4096]{1,0:T(8,128)}, u32[]{:S(2)}) copy-start(f32[8,4096]{1,0:T(8,128)} %get-tuple-element.5) | copy-start | bytes 393220

commit v2 on v1

v2 whole, which is shorter than its diff:
```python
import functools
import math

import jax
import jax.numpy as jnp
import numpy as np
from jax import lax
from jax.experimental import pallas as pl
from jax.experimental.pallas import tpu as pltpu
from jax.sharding import PartitionSpec as P

BF = jnp.bfloat16
F32 = jnp.float32
MESH = pl.DeviceIdType.MESH
NT = (((1,), (1,)), ((), ()))

LEAF = 256
RANK = 64
RHS = 8
PER = 16
NEAR = 16
FARL = 32
FARM = 16
FART = 3
GROUPS = 8
GSIZE = 16
LEAVES = 2048
WIN = 3 * PER
PIECES = 48
TILES1 = 2 + PER
TILES2 = 1 + PER // 2
PACKED = 3 * PER * LEAF // 8

LOG2E = math.log2(math.e)
KAPPA = 0.75 * LOG2E * LOG2E
FACTOR = math.e * math.log(2.0)
TINY = 1e-30


def morton_table():
    ids = np.arange(LEAVES)
    coords = [np.zeros_like(ids) for _ in range(3)]
    for bit in range(30):
        coords[bit % 3] += ((ids >> bit) & 1) << (bit // 3)
    packed = coords[0] + 256 * coords[1] + 65536 * coords[2]
    return np.pad(packed, (PER, PER)).astype(np.int32)


def tangent_tables():
    mean = 0.75 * (np.arange(512) + 0.5)
    s = np.sqrt(mean)
    beta = 0.5 * np.exp(-s) / (LOG2E * LOG2E) / FACTOR
    alpha = -(1 + s) * np.exp(-s) / FACTOR - beta * mean * LOG2E * LOG2E
    return alpha.astype(np.float32), beta.astype(np.float32)


def rounded(x):
    return x.astype(BF).astype(F32)


def split2(x):
    high = rounded(x)
    return jnp.concatenate([high, x - high], axis=0).astype(BF)


def split3(x):
    first = rounded(x)
    rest = x - first
    second = rounded(rest)
    return first, second, rounded(rest - second)


def source_pieces(w):
    a, b, c = split3(w)
    return jnp.concatenate([a, b, a, b, c, a], axis=0)


def target_pieces(u):
    a, b, c = split3(u)
    return jnp.concatenate([a, a, b, b, a, c], axis=0)


def rows_of(shape):
    return lax.broadcasted_iota(jnp.int32, shape, 0)


def source_rows(x):
    row = rows_of(x.shape)
    x = jnp.where(row < 3, x, 0.0)
    norm = KAPPA * jnp.sum(x * x, axis=0, keepdims=True)
    return jnp.where(row == 3, norm, jnp.where(row == 4, 1.0, x))


def target_rows(x):
    row = rows_of(x.shape)
    x = jnp.where(row < 3, x, 0.0)
    norm = KAPPA * jnp.sum(x * x, axis=0, keepdims=True)
    return jnp.where(row == 4, norm, jnp.where(row == 3, 1.0, (-2.0 * KAPPA) * x))


def kernel_value(q):
    q = jnp.maximum(q, TINY)
    y = -LOG2E - q * lax.rsqrt(q)
    return y * jnp.exp2(y)


def halves(x):
    high = x.astype(BF)
    return high, (x - high.astype(F32)).astype(BF)


def dot(a, b):
    return jnp.dot(a, b, preferred_element_type=F32)


def dot_nt(a, b):
    return lax.dot_general(a, b, NT, preferred_element_type=F32)


def fold(x):
    return x[:RHS] + x[RHS:]


def body(
    points,
    rhs,
    start,
    leaf_skel,
    mid_skel,
    top_skel,
    basis,
    transfer,
    mid_transfer,
    noise,
    near,
    near_count,
    far_leaf,
    far_count,
    far_mid,
    far_top,
    corners,
    alphas,
    betas,
    first,
    image,
    step,
    remainder,
    far_high,
    far_low,
    mid_high,
    mid_low,
    top_high,
    top_low,
    halo1,
    halo2,
    gather1,
    gather2,
    all1,
    all2,
    sums1,
    sums2,
    field,
    wfeat,
    ufeat,
    urows,
    moments,
    skel_rows,
    tangent_a,
    tangent_b,
    skel_feat,
    mid_feat,
    top_feat,
    top_tiles,
    basis_high,
    basis_low,
    transfer2,
    near_acc,
    local,
    halo_send,
    halo_recv,
    coef_send,
    coef_recv,
    all_send,
    all_recv,
    sum_send,
    sum_recv,
    tot_send,
    tot_recv,
):
    g = lax.axis_index("grp")
    i = lax.axis_index("leaf")
    lane = lax.broadcasted_iota(jnp.int32, (RHS, 128), 1)
    low_lanes = lane < RANK

    def peer_leaf(k):
        return (g, lax.rem(i + k, GSIZE))

    def peer_grp(k):
        return (lax.rem(g + k, GROUPS), i)

    up = i + 1
    down = i + GSIZE - 1
    after = (lax.rem(g + lax.div(up, GSIZE), GROUPS), lax.rem(up, GSIZE))
    before = (lax.rem(g + GROUPS - 1 + lax.div(down, GSIZE), GROUPS), lax.rem(down, GSIZE))

    barrier = pltpu.get_barrier_semaphore()
    partners = (
        [peer_leaf(k) for k in range(1, GSIZE)]
        + [peer_grp(k) for k in range(1, GROUPS)]
        + [after, before]
    )
    for partner in partners:
        pl.semaphore_signal(barrier, inc=1, device_id=partner, device_id_type=MESH)

    def remote(src, dst, send, recv, device):
        return pltpu.make_async_remote_copy(
            src_ref=src,
            dst_ref=dst,
            send_sem=send,
            recv_sem=recv,
            device_id=device,
            device_id_type=MESH,
        )

    def halo_copies(window, phase, *where):
        own, low, high = (window.at[(block,) + where] for block in (1, 0, 2))
        return [
            remote(own, low, halo_send.at[phase, 0], halo_recv.at[phase, 0], after),
            remote(own, high, halo_send.at[phase, 1], halo_recv.at[phase, 1], before),
        ]

    def leaf_copies(buffer, send, recv, phase):
        own = buffer.at[i]
        return [
            remote(own, own, send.at[phase, k], recv.at[phase, i], peer_leaf(k))
            for k in range(1, GSIZE)
        ]

    def wait_leaf(buffer, send, recv, phase):
        for k in range(1, GSIZE):
            src = lax.rem(i + k, GSIZE)
            theirs = buffer.at[src]
            remote(theirs, theirs, send.at[phase, k], recv.at[phase, src], peer_leaf(k)).wait_recv()

    def grp_copies(buffer, send, recv, phase):
        return [
            remote(buffer.at[g], buffer.at[g], send.at[phase, k], recv.at[phase, g], peer_grp(k))
            for k in range(1, GROUPS)
        ]

    def wait_grp(buffer, send, recv, phase):
        for k in range(1, GROUPS):
            src = lax.rem(g + k, GROUPS)
            remote(
                buffer.at[src], buffer.at[src], send.at[phase, k], recv.at[phase, src], peer_grp(k)
            ).wait_recv()

    pending = []

    def launch(copies):
        for copy in copies:
            copy.start()
        pending.extend(copies)

    def coefficients(read, tiles, first_tile):
        total = jnp.zeros((2 * RHS, RANK), F32)
        for p in range(PER // 2):
            parts = []
            for side in range(2):
                leaf = 2 * p + side
                v = split2(read(leaf))
                field[PER + leaf] = v
                parts.append(fold(dot_nt(v, basis_high[leaf]) + dot_nt(v, basis_low[leaf])))
            tile = jnp.concatenate(parts, axis=1)
            tiles[first_tile + p] = tile
            c = split2(tile)
            for part in range(2):
                total += dot_nt(c, transfer2[part, :, 128 * p : 128 * (p + 1)])
        mid = fold(total)
        m = split2(mid)
        high, low = halves(mid_transfer[0])
        top = fold(dot_nt(m, high) + dot_nt(m, low))
        tiles[0] = jnp.concatenate([mid, top], axis=1)

    def column(leaf):
        return pl.ds(pl.multiple_of(leaf * LEAF, LEAF), LEAF)

    width, span = PER * LEAF, PACKED // 3
    halo1[1, :, 0:width] = start[...]
    for c in range(3):
        for r in range(8):
            halo1[1, r : r + 1, width + c * span : width + (c + 1) * span] = points[
                c : c + 1, r * span : (r + 1) * span
            ]
    for leaf in range(PER):
        high, low = halves(basis[leaf])
        basis_high[leaf] = high
        basis_low[leaf] = low
    for p in range(PER // 2):
        both = jnp.concatenate([transfer[2 * p], transfer[2 * p + 1]], axis=1)
        high, low = halves(both)
        transfer2[0, :, 128 * p : 128 * (p + 1)] = high
        transfer2[1, :, 128 * p : 128 * (p + 1)] = low
    pl.semaphore_wait(barrier, len(partners))
    launch(halo_copies(halo1, 0))

    own_gather = gather1.at[i]
    own_skel = []
    for p in range(PER // 2):
        tile = jnp.concatenate(
            [leaf_skel[:, 128 * p : 128 * (p + 1)], jnp.zeros((5, 128), F32)], axis=0
        )
        own_skel.append(tile)
        own_gather[2 + PER // 2 + p] = tile
    own_gather[1] = jnp.zeros((8, 128), F32)
    own_gather[1, 0:3, 0:RANK] = mid_skel[...]
    coefficients(lambda leaf: start[:, LEAF * leaf : LEAF * (leaf + 1)], own_gather, 2)
    launch(leaf_copies(gather1, coef_send, coef_recv, 0))

    centre = jnp.concatenate([jnp.floor(points[:, 0:1]), jnp.zeros((5, 1), F32)], axis=0)
    device = g * GSIZE + i
    base = device * PER

    def leaf_points(block, l):
        per_row = span // LEAF
        row, place = lax.div(l, per_row), lax.rem(l, per_row) * LEAF
        out = jnp.zeros((8, LEAF), F32)
        for c in range(3):
            cols = pl.ds(pl.multiple_of(width + c * span + place, LEAF), LEAF)
            out = jnp.where(rows_of((8, LEAF)) == c, halo1[block, pl.ds(row, 1), cols], out)
        return out

    def window_features(leaf, block, place):
        x = leaf_points(block, place) - centre
        wfeat[leaf] = source_pieces(source_rows(x)).T.astype(BF)
        return x

    def tangents(l):
        a = corners[base + PER + l] + 0x202020
        count = near_count[l]
        for s in range(NEAR):
            d = a - corners[base + near[l, s]]
            dx = (d & 255) - 32
            dy = ((d >> 8) & 255) - 32
            dz = (d >> 16) - 32
            d2 = jnp.minimum(dx * dx + dy * dy + dz * dz, 511)
            live = s < count
            tangent_a[l, s] = jnp.where(live, alphas[d2], 0.0)
            tangent_b[l, s] = jnp.where(live, betas[d2], 0.0)

    def own_features(n, carry):
        for t in range(4):
            l = 4 * n + t
            x = window_features(PER + l, 1, l)
            u = target_rows(x)
            urows[l] = u
            ufeat[l] = target_pieces(u).astype(BF)
            tangents(l)
        return carry

    lax.fori_loop(0, PER // 4, own_features, 0)
    for p in range(PER // 2):
        u = target_pieces(target_rows(own_skel[p] - centre))
        skel_feat[128 * p : 128 * (p + 1), :] = u.T.astype(BF)
    u = target_pieces(target_rows(own_gather[1] - centre))
    mid_feat[...] = u.T.astype(BF)
    for p in range(GROUPS // 2):
        top_tiles[p] = jnp.concatenate(
            [top_skel[:, 128 * p : 128 * (p + 1)], jnp.zeros((5, 128), F32)], axis=0
        )
    tile = top_tiles[lax.div(g, 2)]
    tile = jnp.where(lax.rem(g, 2) == 0, tile, pltpu.roll(tile, RANK, 1))
    top_feat[...] = target_pieces(target_rows(tile - centre)).T.astype(BF)

    def field_moments(first_leaf):
        lane8 = lax.broadcasted_iota(jnp.int32, (RHS, 8), 1)

        def some(n, carry):
            for t in range(8):
                leaf = first_leaf + 8 * n + t
                r = fold(dot(field[leaf], wfeat[leaf]))
                m = r[:, 0:8] + r[:, 8:16] + r[:, 32:40]
                moments[leaf, 0] = m
                moments[leaf, 1] = jnp.where(lane8 == 3, m[:, 4:5], 0.0)
            return carry

        lax.fori_loop(0, PER // 8, some, 0)

    field_moments(PER)
    for copy in halo_copies(halo1, 0):
        copy.wait_recv()

    def edge_features(n, carry):
        for t in range(4):
            l = 4 * n + t
            for block in (0, 2):
                leaf = block * PER + l
                window_features(leaf, block, l)
                field[leaf] = split2(halo1[block, :, column(l)])
        return carry

    lax.fori_loop(0, PER // 4, edge_features, 0)
    field_moments(0)
    field_moments(2 * PER)

    def evaluate(l):
        feat = ufeat[l]
        for c in range(0, LEAF, 64):
            for t in range(NEAR):
                q = dot(wfeat[near[l, t], c : c + 64, :], feat)
                r = kernel_value(q) - (q * tangent_b[l, t] + tangent_a[l, t])
                row = (l * NEAR + t) * LEAF + c
                remainder[pl.ds(pl.multiple_of(row, 64), 64), :] = r.astype(BF)

    def multiply(l):
        cols = []
        live = near_count[l]
        for t in range(NEAR):
            v = field[near[l, t]]
            cols.append(jnp.where(t < live, v, jnp.zeros_like(v)))
        row = pl.multiple_of(l * NEAR * LEAF, LEAF)
        near_acc[l] = dot(jnp.concatenate(cols, axis=1), remainder[pl.ds(row, NEAR * LEAF), :])

    def tangent_part(l):
        total = jnp.zeros((RHS, 8), F32)
        for s in range(NEAR):
            j = near[l, s]
            total += tangent_b[l, s] * moments[j, 0] + tangent_a[l, s] * moments[j, 1]
        out = total[:, 0:1] * urows[l, 0:1, :]
        for k in range(1, 5):
            out += total[:, k : k + 1] * urows[l, k : k + 1, :]
        return out

    remainder[(PER - 1) * NEAR * LEAF :, :] = jnp.zeros((NEAR * LEAF, LEAF), BF)

    def near_step(l, carry):
        multiply(lax.rem(l + PER - 1, PER))
        evaluate(l)
        return carry

    lax.fori_loop(0, PER // 2, near_step, 0)
    wait_leaf(gather1, coef_send, coef_recv, 0)
    for m in range(GSIZE):
        all1[g, m] = gather1[m, 0:2]
    launch(grp_copies(all1, all_send, all_recv, 0))
    lax.fori_loop(PER // 2, PER, near_step, 0)
    multiply(PER - 1)

    def moved(tile, index, want):
        return jnp.where((index & 1) == want, tile, pltpu.roll(tile, RANK, 1))

    def joined(first_tile, second_tile):
        return jnp.where(low_lanes, first_tile, second_tile)

    def far_tiles(feat, rows):
        return halves(kernel_value(dot(feat, source_pieces(rows).astype(BF))))

    def skeleton_rows(n, carry):
        for t in range(PER // 2):
            skel_rows[n * (PER // 2) + t] = source_rows(gather1[n, 2 + PER // 2 + t] - centre)
        return carry

    def far_matrix(lp, carry):
        for side in range(4):
            l = 4 * lp + side
            feat = skel_feat[pl.ds(pl.multiple_of(l * RANK, RANK), RANK), :]
            for p in range(FARL // 2):
                j1, j2 = far_leaf[l, 2 * p], far_leaf[l, 2 * p + 1]
                rows = joined(
                    moved(skel_rows[j1 >> 1], j1, 0), moved(skel_rows[j2 >> 1], j2, 1)
                )
                high, low = far_tiles(feat, rows)
                far_high[l, :, 128 * p : 128 * (p + 1)] = high
                far_low[l, :, 128 * p : 128 * (p + 1)] = low
        return carry

    def far_leaves(read):
        def some(n, carry):
            for q in range(2):
                lp = 2 * n + q
                parts = []
                for side in range(2):
                    l = 2 * lp + side
                    count = far_count[l]
                    cols = []
                    for p in range(FARL // 2):
                        s = 2 * p
                        j1, j2 = far_leaf[l, s], far_leaf[l, s + 1]
                        tile = joined(moved(read(j1), j1, 0), moved(read(j2), j2, 1))
                        slot = s + jnp.where(low_lanes, 0, 1)
                        cols.append(split2(jnp.where(slot < count, tile, 0.0)))
                    c = jnp.concatenate(cols, axis=1)
                    parts.append(dot_nt(far_high[l], c) + dot_nt(far_low[l], c))
                local[lp] = -FACTOR * fold(jnp.concatenate(parts, axis=0).T)
            return carry

        lax.fori_loop(0, PER // 4, some, 0)

    def upper_matrix(buffer):
        def read_mid(m):
            return source_rows(buffer[m >> 4, m & 15, 1] - centre)

        for p in range(FARM // 2):
            one, two = read_mid(far_mid[0, 2 * p]), read_mid(far_mid[0, 2 * p + 1])
            high, low = far_tiles(mid_feat[0:RANK, :], joined(one, pltpu.roll(two, RANK, 1)))
            mid_high[:, 128 * p : 128 * (p + 1)] = high
            mid_low[:, 128 * p : 128 * (p + 1)] = low

        def read_top(j, want):
            return moved(source_rows(top_tiles[j >> 1] - centre), j, want)

        for p in range(2):
            j1 = far_top[0, 2 * p]
            j2 = far_top[0, min(2 * p + 1, FART - 1)]
            high, low = far_tiles(top_feat[0:RANK, :], joined(read_top(j1, 0), read_top(j2, 1)))
            top_high[:, 128 * p : 128 * (p + 1)] = high
            top_low[:, 128 * p : 128 * (p + 1)] = low

    def upper_local(read):
        cols = []
        for p in range(FARM // 2):
            m1, m2 = far_mid[0, 2 * p], far_mid[0, 2 * p + 1]
            one, two = read(m1 >> 4, m1 & 15), read(m2 >> 4, m2 & 15)
            cols.append(split2(joined(one, pltpu.roll(two, RANK, 1))))
        c = jnp.concatenate(cols, axis=1)
        mid_far = -FACTOR * fold(dot_nt(c, mid_high[...]) + dot_nt(c, mid_low[...]))

        def top(j):
            total = read(j, 0)
            for m in range(1, GSIZE):
                total += read(j, m)
            return total

        t0, t1, t2 = (top(far_top[0, s]) for s in range(FART))
        cols = [
            split2(joined(pltpu.roll(t0, RANK, 1), t1)),
            split2(joined(pltpu.roll(t2, RANK, 1), jnp.zeros((RHS, 128), F32))),
        ]
        c = jnp.concatenate(cols, axis=1)
        top_far = -FACTOR * fold(dot_nt(c, top_high[...]) + dot_nt(c, top_low[...]))
        high, low = halves(mid_transfer[0])
        t = split2(top_far)
        return mid_far + fold(dot(t, high) + dot(t, low))

    def down(read_mid):
        m = split2(upper_local(read_mid))
        for p in range(PER // 2):
            down_part = sum(dot(m, transfer2[part, :, 128 * p : 128 * (p + 1)]) for part in range(2))
            local[p] += fold(down_part)

    def finish(n, store):
        for t in range(4):
            l = 4 * n + t
            tile = local[2 * n + t // 2]
            c = split2(tile[:, RANK * (t % 2) : RANK * (t % 2 + 1)])
            far = fold(dot(c, basis_high[l]) + dot(c, basis_low[l]))
            near_part = -FACTOR * (fold(near_acc[l]) + tangent_part(l))
            store(l, near_part + far)

    lax.fori_loop(0, GSIZE, skeleton_rows, 0)
    lax.fori_loop(0, PER // 4, far_matrix, 0)
    far_leaves(lambda j: gather1[j >> 4, 2 + ((j >> 1) & 7)])
    wait_grp(all1, all_send, all_recv, 0)
    upper_matrix(all1)
    noise_value = noise[0]

    def first_leaves(n, carry):
        def store(l, value):
            cols = column(l)
            r = rhs[:, cols] - (noise_value * start[:, cols] + value)
            first[:, cols] = r
            halo2[1, :, cols] = r

        finish(n, store)
        return carry

    left, right = (slice(None), slice(0, width // 2)), (slice(None), slice(width // 2, width))
    down(lambda a, b: all1[a, b, 0])
    lax.fori_loop(0, PER // 8, first_leaves, 0)
    launch(halo_copies(halo2, 1, *left))
    lax.fori_loop(PER // 8, PER // 4, first_leaves, 0)
    launch(halo_copies(halo2, 2, *right))

    coefficients(lambda leaf: first[:, LEAF * leaf : LEAF * (leaf + 1)], gather2.at[i], 1)
    launch(leaf_copies(gather2, coef_send, coef_recv, 1))
    field_moments(PER)
    for copy in halo_copies(halo2, 1, *left) + halo_copies(halo2, 2, *right):
        copy.wait_recv()

    def edge_fields(n, carry):
        for t in range(4):
            l = 4 * n + t
            for block in (0, 2):
                field[block * PER + l] = split2(halo2[block, :, column(l)])
        return carry

    lax.fori_loop(0, PER // 4, edge_fields, 0)
    field_moments(0)
    field_moments(2 * PER)

    def near_again(l, carry):
        multiply(l)
        return carry

    lax.fori_loop(0, PER // 2, near_again, 0)
    wait_leaf(gather2, coef_send, coef_recv, 1)
    for m in range(GSIZE):
        all2[g, m] = gather2[m, 0]
    launch(grp_copies(all2, all_send, all_recv, 1))
    lax.fori_loop(PER // 2, PER, near_again, 0)
    far_leaves(lambda j: gather2[j >> 4, 1 + ((j >> 1) & 7)])
    wait_grp(all2, all_send, all_recv, 1)

    def image_leaves(n, carry):
        def store(l, value):
            cols = column(l)
            image[:, cols] = noise_value * first[:, cols] + value

        finish(n, store)
        return carry

    down(lambda a, b: all2[a, b])
    lax.fori_loop(0, PER // 4, image_leaves, 0)

    dots = jnp.zeros((RHS, LEAF), F32)
    squares = jnp.zeros((RHS, LEAF), F32)
    for l in range(PER):
        cols = slice(LEAF * l, LEAF * (l + 1))
        y = image[:, cols]
        dots += first[:, cols] * y
        squares += y * y
    sums1[i] = jnp.where(
        low_lanes,
        jnp.sum(dots, axis=1, keepdims=True),
        jnp.sum(squares, axis=1, keepdims=True),
    )
    launch(leaf_copies(sums1, sum_send, sum_recv, 0))
    wait_leaf(sums1, sum_send, sum_recv, 0)
    total = sums1[0]
    for k in range(1, GSIZE):
        total += sums1[k]
    sums2[g] = total
    launch(grp_copies(sums2, tot_send, tot_recv, 0))
    wait_grp(sums2, tot_send, tot_recv, 0)
    total = sums2[0]
    for k in range(1, GROUPS):
        total += sums2[k]
    total = total / (LEAVES * LEAF)
    alpha = total[:, 0:1] / (total[:, RANK : RANK + 1] + 1e-6)
    step[...] = jnp.broadcast_to(alpha, (RHS, 128))
    for copy in pending:
        copy.wait_send()


def shards(*args):
    smem = pl.BlockSpec(memory_space=pltpu.SMEM)
    vmem = pl.BlockSpec(memory_space=pltpu.VMEM)
    alphas, betas = tangent_tables()
    tables = (jnp.asarray(morton_table()), jnp.asarray(alphas), jnp.asarray(betas))
    out = jax.ShapeDtypeStruct((RHS, PER * LEAF), F32)
    tile = (8, 128)

    def buffer(shape, dtype=F32):
        return pltpu.VMEM(shape, dtype)

    def sems(*shape):
        return pltpu.SemaphoreType.DMA(shape)

    scratch = [
        buffer((PER * NEAR * LEAF, LEAF), BF),
        buffer((PER, RANK, FARL * RANK), BF),
        buffer((PER, RANK, FARL * RANK), BF),
        buffer((RANK, FARM * RANK), BF),
        buffer((RANK, FARM * RANK), BF),
        buffer((RANK, 4 * RANK), BF),
        buffer((RANK, 4 * RANK), BF),
        buffer((3, 8, PER * LEAF + PACKED)),
        buffer((3, 8, PER * LEAF)),
        buffer((GSIZE, TILES1) + tile),
        buffer((GSIZE, TILES2) + tile),
        buffer((GROUPS, GSIZE, 2) + tile),
        buffer((GROUPS, GSIZE) + tile),
        buffer((GSIZE,) + tile),
        buffer((GROUPS,) + tile),
        buffer((WIN, 2 * RHS, LEAF), BF),
        buffer((WIN, LEAF, PIECES), BF),
        buffer((PER, PIECES, LEAF), BF),
        buffer((PER, 8, LEAF)),
        buffer((WIN, 2, RHS, 8)),
        buffer((GSIZE * PER // 2,) + tile),
        pltpu.SMEM((PER, NEAR), F32),
        pltpu.SMEM((PER, NEAR), F32),
        buffer((PER * RANK, PIECES), BF),
        buffer((128, PIECES), BF),
        buffer((128, PIECES), BF),
        buffer((GROUPS // 2,) + tile),
        buffer((PER, RANK, LEAF), BF),
        buffer((PER, RANK, LEAF), BF),
        buffer((2, RANK, PER * RANK), BF),
        buffer((PER, 2 * RHS, LEAF)),
        buffer((PER // 2,) + tile),
        sems(3, 2),
        sems(3, 2),
        sems(2, GSIZE),
        sems(2, GSIZE),
        sems(2, GROUPS),
        sems(2, GROUPS),
        sems(1, GSIZE),
        sems(1, GSIZE),
        sems(1, GROUPS),
        sems(1, GROUPS),
    ]
    first, image, step = pl.pallas_call(
        body,
        out_shape=(out, out, jax.ShapeDtypeStruct(tile, F32)),
        in_specs=[vmem] * 9 + [smem] * 10,
        out_specs=(vmem, vmem, vmem),
        scratch_shapes=scratch,
        compiler_params=pltpu.CompilerParams(
            collective_id=0, has_side_effects=True, vmem_limit_bytes=61 << 20
        ),
    )(*args, *tables)
    alpha = step[:, 0:1]
    return args[2] + alpha * first, first - alpha * image


def solution(mesh):
    columns = P(None, ("grp", "leaf"))
    blocks = P(("grp", "leaf"), None, None)
    lists = P(("grp", "leaf"), None)
    return jax.shard_map(
        shards,
        mesh=mesh,
        in_specs=(
            columns,
            columns,
            columns,
            columns,
            columns,
            P(),
            blocks,
            blocks,
            blocks,
            P(),
            lists,
            P(("grp", "leaf")),
            lists,
            P(("grp", "leaf")),
            lists,
            P("grp", None),
        ),
        out_specs=(columns, columns),
        check_vma=False,
    )
```

time: 121 us -> 97.2 us (0.80)
  Pallas kernels: 117 us -> 93.1 us
  other arithmetic: 0 us -> 1.76 us
  local copies, waits for them, and re-layouts: 2.26 us -> 0.79 us
    pallas_call x1, Pallas kernels: 117 us -> 93.1 us  [shards(): pl.pallas_call(body, out_shape=(out, out, jax.ShapeDtypeStruct(tile, F32)...]
    sub x0 -> x1, other arithmetic: none -> 1.76 us  [shards(): return (args[2] + alpha * first, first - alpha * image)]
    unnamed x4, local copies, waits for them, and re-layouts: 2.26 us -> 0.68 us
where the time goes in v2:
time: 97.2 us; the launch traced here: 97 us
  Pallas kernels  93.1 us (96%)
  other arithmetic  1.76 us (2%)
  between operations  1.31 us (1%)
    pallas_call x1, Pallas kernels, shards(): pl.pallas_call(body, out_shape=(out, out, jax.ShapeDtypeStruct(tile, F32)...  93.1 us

profile of v2, /device:TPU:1, one launch (start us, length us, event | category | flops | bytes accessed | tf_op | source)
XLA Modules:
  0.0 97.0 jit_solution(5374151667793117300)
XLA Ops:
  1.3 0.0 copy-start
  1.3 93.1 %shard_map.194 = (f32[8,4096]{1,0:T(8,128)}, f32[8,4096]{1,0:T(8,128)}, f32[8,128]{1,0:T(8,128)}) custom-call(f32[3,4096]{1,0:T(4,128)} %points.1, f32[8,4096]{1,0:T(8,128)} %rhs.2, f32[8,4096]{1,0:T(8,128)} %start.1, f32[3,1024]{1,0:T(4,128)} %leaf_skel.1, f32[3,64]{1,0:T(4,128)} %mid_skel.1, f32[3,512]{1,0:T(4,128)} %top_skel.1, f32[16,64,256]{2,1,0:T(8,128)} %basis.1, ...), custom_call_target="tpu_custom_call" | custom-call | tf_op jit(solution)/shard_map/pallas_call | solution.py:713
  94.4 0.0 copy-start.1
  94.4 0.7 copy-done.1
  95.1 0.1 slice_reduce_fusion
  95.2 0.0 copy-done
  95.2 1.8 %multiply_subtract_fusion = (f32[8,4096]{1,0:T(8,128)}, f32[8,4096]{1,0:T(8,128)}) fusion(f32[8,4096]{1,0:T(8,128)} %get-tuple-element.6, f32[8,4096]{1,0:T(8,128)} %get-tuple-element.7, f32[8]{0:T(128)S(1)} %slice_reduce_fusion, f32[8,4096]{1,0:T(8,128)S(1)} %copy-done), kind=kLoop, calls=%fused_computation | loop fusion | flops 131072 | bytes 655392 | tf_op jit(solution)/shard_map/sub | solution.py:724
Async XLA Ops:
  1.3 93.9 %copy-start = (f32[8,4096]{1,0:T(8,128)S(1)}, f32[8,4096]{1,0:T(8,128)}, u32[]{:S(2)}) copy-start(f32[8,4096]{1,0:T(8,128)} %start.1) | copy-start | bytes 393220
  94.4 0.7 copy-start.1

commit v3 on v2

--- a/solution.py
+++ b/solution.py
@@ -51,6 +51,7 @@
     s = np.sqrt(mean)
     beta = 0.5 * np.exp(-s) / (LOG2E * LOG2E) / FACTOR
     alpha = -(1 + s) * np.exp(-s) / FACTOR - beta * mean * LOG2E * LOG2E
+    alpha = np.append(alpha, -LOG2E)
     return alpha.astype(np.float32), beta.astype(np.float32)
 
 
@@ -98,9 +99,8 @@
     return jnp.where(row == 4, norm, jnp.where(row == 3, 1.0, (-2.0 * KAPPA) * x))
 
 
-def kernel_value(q):
-    q = jnp.maximum(q, TINY)
-    y = -LOG2E - q * lax.rsqrt(q)
+def kernel_value(q, shift):
+    y = shift - q * lax.rsqrt(q)
     return y * jnp.exp2(y)
 
 
@@ -144,7 +144,8 @@
     first,
     image,
     step,
-    remainder,
+    remainder0,
+    remainder1,
     far_high,
     far_low,
     mid_high,
@@ -191,6 +192,7 @@
     i = lax.axis_index("leaf")
     lane = lax.broadcasted_iota(jnp.int32, (RHS, 128), 1)
     low_lanes = lane < RANK
+    tile_shape = (RHS, 128)
 
     def peer_leaf(k):
         return (g, lax.rem(i + k, GSIZE))
@@ -403,23 +405,28 @@
     field_moments(0)
     field_moments(2 * PER)
 
-    def evaluate(l):
+    shift = alphas[512]
+    remainders = (remainder0, remainder1)
+
+    def evaluate(n, side):
+        l = 2 * n + side
         feat = ufeat[l]
         for c in range(0, LEAF, 64):
             for t in range(NEAR):
-                q = dot(wfeat[near[l, t], c : c + 64, :], feat)
-                r = kernel_value(q) - (q * tangent_b[l, t] + tangent_a[l, t])
-                row = (l * NEAR + t) * LEAF + c
-                remainder[pl.ds(pl.multiple_of(row, 64), 64), :] = r.astype(BF)
-
-    def multiply(l):
+                q = jnp.maximum(dot(wfeat[near[l, t], c : c + 64, :], feat), TINY)
+                r = kernel_value(q, shift) - (q * tangent_b[l, t] + tangent_a[l, t])
+                row = (n * NEAR + t) * LEAF + c
+                remainders[side][pl.ds(pl.multiple_of(row, 64), 64), :] = r.astype(BF)
+
+    def multiply(n, side):
+        l = 2 * n + side
         cols = []
         live = near_count[l]
         for t in range(NEAR):
             v = field[near[l, t]]
             cols.append(jnp.where(t < live, v, jnp.zeros_like(v)))
-        row = pl.multiple_of(l * NEAR * LEAF, LEAF)
-        near_acc[l] = dot(jnp.concatenate(cols, axis=1), remainder[pl.ds(row, NEAR * LEAF), :])
+        rows = pl.ds(pl.multiple_of(n * NEAR * LEAF, LEAF), NEAR * LEAF)
+        near_acc[l] = dot(jnp.concatenate(cols, axis=1), remainders[side][rows, :])
 
     def tangent_part(l):
         total = jnp.zeros((RHS, 8), F32)
@@ -431,20 +438,22 @@
             out += total[:, k : k + 1] * urows[l, k : k + 1, :]
         return out
 
-    remainder[(PER - 1) * NEAR * LEAF :, :] = jnp.zeros((NEAR * LEAF, LEAF), BF)
-
-    def near_step(l, carry):
-        multiply(lax.rem(l + PER - 1, PER))
-        evaluate(l)
-        return carry
-
-    lax.fori_loop(0, PER // 2, near_step, 0)
+    remainder1[(PER // 2 - 1) * NEAR * LEAF :, :] = jnp.zeros((NEAR * LEAF, LEAF), BF)
+
+    def near_step(n, carry):
+        multiply(lax.rem(n + PER // 2 - 1, PER // 2), 1)
+        evaluate(n, 0)
+        multiply(n, 0)
+        evaluate(n, 1)
+        return carry
+
+    lax.fori_loop(0, PER // 4, near_step, 0)
     wait_leaf(gather1, coef_send, coef_recv, 0)
     for m in range(GSIZE):
         all1[g, m] = gather1[m, 0:2]
     launch(grp_copies(all1, all_send, all_recv, 0))
-    lax.fori_loop(PER // 2, PER, near_step, 0)
-    multiply(PER - 1)
+    lax.fori_loop(PER // 4, PER // 2, near_step, 0)
+    multiply(PER // 2 - 1, 1)
 
     def moved(tile, index, want):
         return jnp.where((index & 1) == want, tile, pltpu.roll(tile, RANK, 1))
@@ -453,7 +462,8 @@
         return jnp.where(low_lanes, first_tile, second_tile)
 
     def far_tiles(feat, rows):
-        return halves(kernel_value(dot(feat, source_pieces(rows).astype(BF))))
+        q = jnp.maximum(dot(feat, source_pieces(rows).astype(BF)), TINY)
+        return halves(kernel_value(q, shift))
 
     def skeleton_rows(n, carry):
         for t in range(PER // 2):
@@ -516,22 +526,15 @@
             top_high[:, 128 * p : 128 * (p + 1)] = high
             top_low[:, 128 * p : 128 * (p + 1)] = low
 
-    def upper_local(read):
+    def upper_local(read, read_top):
         cols = []
         for p in range(FARM // 2):
             m1, m2 = far_mid[0, 2 * p], far_mid[0, 2 * p + 1]
-            one, two = read(m1 >> 4, m1 & 15), read(m2 >> 4, m2 & 15)
-            cols.append(split2(joined(one, pltpu.roll(two, RANK, 1))))
+            cols.append(split2(joined(read(m1, 0), read(m2, 1))))
         c = jnp.concatenate(cols, axis=1)
         mid_far = -FACTOR * fold(dot_nt(c, mid_high[...]) + dot_nt(c, mid_low[...]))
 
-        def top(j):
-            total = read(j, 0)
-            for m in range(1, GSIZE):
-                total += read(j, m)
-            return total
-
-        t0, t1, t2 = (top(far_top[0, s]) for s in range(FART))
+        t0, t1, t2 = (read_top(far_top[0, s]) for s in range(FART))
         cols = [
             split2(joined(pltpu.roll(t0, RANK, 1), t1)),
             split2(joined(pltpu.roll(t2, RANK, 1), jnp.zeros((RHS, 128), F32))),
@@ -542,8 +545,8 @@
         t = split2(top_far)
         return mid_far + fold(dot(t, high) + dot(t, low))
 
-    def down(read_mid):
-        m = split2(upper_local(read_mid))
+    def down(read_mid, read_top):
+        m = split2(upper_local(read_mid, read_top))
         for p in range(PER // 2):
             down_part = sum(dot(m, transfer2[part, :, 128 * p : 128 * (p + 1)]) for part in range(2))
             local[p] += fold(down_part)
@@ -575,7 +578,17 @@
         return carry
 
     left, right = (slice(None), slice(0, width // 2)), (slice(None), slice(width // 2, width))
-    down(lambda a, b: all1[a, b, 0])
+    def mid1(m, want):
+        tile = all1[m >> 4, m & 15, 0]
+        return pltpu.roll(tile, RANK, 1) if want else tile
+
+    def top1(j):
+        total = all1[j, 0, 0]
+        for m in range(1, GSIZE):
+            total += all1[j, m, 0]
+        return total
+
+    down(mid1, top1)
     lax.fori_loop(0, PER // 8, first_leaves, 0)
     launch(halo_copies(halo2, 1, *left))
     lax.fori_loop(PER // 8, PER // 4, first_leaves, 0)
@@ -598,16 +611,21 @@
     field_moments(0)
     field_moments(2 * PER)
 
-    def near_again(l, carry):
-        multiply(l)
-        return carry
-
-    lax.fori_loop(0, PER // 2, near_again, 0)
+    def near_again(n, carry):
+        multiply(n, 0)
+        multiply(n, 1)
+        return carry
+
+    lax.fori_loop(0, PER // 2 - 2, near_again, 0)
     wait_leaf(gather2, coef_send, coef_recv, 1)
-    for m in range(GSIZE):
-        all2[g, m] = gather2[m, 0]
+    group_top = jnp.zeros(tile_shape, F32)
+    for p in range(GSIZE // 2):
+        one, two = gather2[2 * p, 0], gather2[2 * p + 1, 0]
+        all2[g, p] = joined(one, pltpu.roll(two, RANK, 1))
+        group_top += one + two
+    all2[g, GSIZE // 2] = group_top
     launch(grp_copies(all2, all_send, all_recv, 1))
-    lax.fori_loop(PER // 2, PER, near_again, 0)
+    lax.fori_loop(PER // 2 - 2, PER // 2, near_again, 0)
     far_leaves(lambda j: gather2[j >> 4, 1 + ((j >> 1) & 7)])
     wait_grp(all2, all_send, all_recv, 1)
 
@@ -619,7 +637,10 @@
         finish(n, store)
         return carry
 
-    down(lambda a, b: all2[a, b])
+    down(
+        lambda m, want: moved(all2[m >> 4, (m & 15) >> 1], m, want),
+        lambda j: all2[j, GSIZE // 2],
+    )
     lax.fori_loop(0, PER // 4, image_leaves, 0)
 
     dots = jnp.zeros((RHS, LEAF), F32)
@@ -667,7 +688,8 @@
         return pltpu.SemaphoreType.DMA(shape)
 
     scratch = [
-        buffer((PER * NEAR * LEAF, LEAF), BF),
+        buffer((PER // 2 * NEAR * LEAF, LEAF), BF),
+        buffer((PER // 2 * NEAR * LEAF, LEAF), BF),
         buffer((PER, RANK, FARL * RANK), BF),
         buffer((PER, RANK, FARL * RANK), BF),
         buffer((RANK, FARM * RANK), BF),
@@ -679,7 +701,7 @@
         buffer((GSIZE, TILES1) + tile),
         buffer((GSIZE, TILES2) + tile),
         buffer((GROUPS, GSIZE, 2) + tile),
-        buffer((GROUPS, GSIZE) + tile),
+        buffer((GROUPS, GSIZE // 2 + 1) + tile),
         buffer((GSIZE,) + tile),
         buffer((GROUPS,) + tile),
         buffer((WIN, 2 * RHS, LEAF), BF),

time: 97.2 us -> 90.9 us (0.935)
  Pallas kernels: 93.1 us -> 86.8 us
    pallas_call x1, Pallas kernels: 93.1 us -> 86.8 us  [shards(): pl.pallas_call(body, out_shape=(out, out, jax.ShapeDtypeStruct(tile, F32)...]
where the time goes in v3:
time: 90.9 us; the launch traced here: 90.7 us
  Pallas kernels  86.8 us (95%)
  other arithmetic  1.76 us (2%)
  between operations  1.31 us (1%)
    pallas_call x1, Pallas kernels, shards(): pl.pallas_call(body, out_shape=(out, out, jax.ShapeDtypeStruct(tile, F32)...  86.8 us

profile of v3, /device:TPU:1, one launch (start us, length us, event | category | flops | bytes accessed | tf_op | source)
XLA Modules:
  0.0 90.7 jit_solution(14369539630025421632)
XLA Ops:
  1.3 0.0 copy-start
  1.3 86.8 %shard_map.194 = (f32[8,4096]{1,0:T(8,128)}, f32[8,4096]{1,0:T(8,128)}, f32[8,128]{1,0:T(8,128)}) custom-call(f32[3,4096]{1,0:T(4,128)} %points.1, f32[8,4096]{1,0:T(8,128)} %rhs.2, f32[8,4096]{1,0:T(8,128)} %start.1, f32[3,1024]{1,0:T(4,128)} %leaf_skel.1, f32[3,64]{1,0:T(4,128)} %mid_skel.1, f32[3,512]{1,0:T(4,128)} %top_skel.1, f32[16,64,256]{2,1,0:T(8,128)} %basis.1, ...), custom_call_target="tpu_custom_call" | custom-call | tf_op jit(solution)/shard_map/pallas_call | solution.py:735
  88.1 0.0 copy-start.1
  88.1 0.7 copy-done.1
  88.8 0.1 slice_reduce_fusion
  88.9 0.0 copy-done
  88.9 1.8 %multiply_subtract_fusion = (f32[8,4096]{1,0:T(8,128)}, f32[8,4096]{1,0:T(8,128)}) fusion(f32[8,4096]{1,0:T(8,128)} %get-tuple-element.6, f32[8,4096]{1,0:T(8,128)} %get-tuple-element.7, f32[8]{0:T(128)S(1)} %slice_reduce_fusion, f32[8,4096]{1,0:T(8,128)S(1)} %copy-done), kind=kLoop, calls=%fused_computation | loop fusion | flops 131072 | bytes 655392 | tf_op jit(solution)/shard_map/sub | solution.py:746
Async XLA Ops:
  1.3 87.6 %copy-start = (f32[8,4096]{1,0:T(8,128)S(1)}, f32[8,4096]{1,0:T(8,128)}, u32[]{:S(2)}) copy-start(f32[8,4096]{1,0:T(8,128)} %start.1) | copy-start | bytes 393220
  88.1 0.7 copy-start.1

commit v4 on v3

--- a/solution.py
+++ b/solution.py
@@ -27,8 +27,8 @@
 LEAVES = 2048
 WIN = 3 * PER
 PIECES = 48
-TILES1 = 2 + PER
-TILES2 = 1 + PER // 2
+TILES1 = 5 + PER // 2
+TILES2 = PER // 2
 PACKED = 3 * PER * LEAF // 8
 
 LOG2E = math.log2(math.e)
@@ -123,13 +123,13 @@
 
 def body(
     points,
-    rhs,
+    rhs_hbm,
     start,
     leaf_skel,
     mid_skel,
     top_skel,
-    basis,
-    transfer,
+    basis_hbm,
+    transfer_hbm,
     mid_transfer,
     noise,
     near,
@@ -156,6 +156,7 @@
     halo2,
     gather1,
     gather2,
+    mids2,
     all1,
     all2,
     sums1,
@@ -177,6 +178,10 @@
     transfer2,
     near_acc,
     local,
+    rhs,
+    basis,
+    transfer,
+    fetch_sem,
     halo_send,
     halo_recv,
     coef_send,
@@ -205,6 +210,14 @@
     after = (lax.rem(g + lax.div(up, GSIZE), GROUPS), lax.rem(up, GSIZE))
     before = (lax.rem(g + GROUPS - 1 + lax.div(down, GSIZE), GROUPS), lax.rem(down, GSIZE))
 
+    fetches = [
+        pltpu.make_async_copy(src, dst, fetch_sem.at[n])
+        for n, (src, dst) in enumerate(
+            ((basis_hbm, basis), (transfer_hbm, transfer), (rhs_hbm, rhs))
+        )
+    ]
+    for copy in fetches:
+        copy.start()
     barrier = pltpu.get_barrier_semaphore()
     partners = (
         [peer_leaf(k) for k in range(1, GSIZE)]
@@ -264,7 +277,7 @@
             copy.start()
         pending.extend(copies)
 
-    def coefficients(read, tiles, first_tile):
+    def coefficients(read, tiles, first_tile, mid_tile):
         total = jnp.zeros((2 * RHS, RANK), F32)
         for p in range(PER // 2):
             parts = []
@@ -282,7 +295,7 @@
         m = split2(mid)
         high, low = halves(mid_transfer[0])
         top = fold(dot_nt(m, high) + dot_nt(m, low))
-        tiles[0] = jnp.concatenate([mid, top], axis=1)
+        mid_tile[...] = jnp.concatenate([mid, top], axis=1)
 
     def column(leaf):
         return pl.ds(pl.multiple_of(leaf * LEAF, LEAF), LEAF)
@@ -294,6 +307,8 @@
             halo1[1, r : r + 1, width + c * span : width + (c + 1) * span] = points[
                 c : c + 1, r * span : (r + 1) * span
             ]
+    for copy in fetches:
+        copy.wait()
     for leaf in range(PER):
         high, low = halves(basis[leaf])
         basis_high[leaf] = high
@@ -313,12 +328,10 @@
             [leaf_skel[:, 128 * p : 128 * (p + 1)], jnp.zeros((5, 128), F32)], axis=0
         )
         own_skel.append(tile)
-        own_gather[2 + PER // 2 + p] = tile
+        own_gather[2 + PER // 2 : 5 + PER // 2, p : p + 1, :] = tile[0:3].reshape(3, 1, 128)
     own_gather[1] = jnp.zeros((8, 128), F32)
     own_gather[1, 0:3, 0:RANK] = mid_skel[...]
-    coefficients(lambda leaf: start[:, LEAF * leaf : LEAF * (leaf + 1)], own_gather, 2)
-    launch(leaf_copies(gather1, coef_send, coef_recv, 0))
-
+    coefficients(lambda leaf: start[:, LEAF * leaf : LEAF * (leaf + 1)], own_gather, 2, own_gather.at[0])
     centre = jnp.concatenate([jnp.floor(points[:, 0:1]), jnp.zeros((5, 1), F32)], axis=0)
     device = g * GSIZE + i
     base = device * PER
@@ -391,6 +404,7 @@
     field_moments(PER)
     for copy in halo_copies(halo1, 0):
         copy.wait_recv()
+    launch(leaf_copies(gather1, coef_send, coef_recv, 0))
 
     def edge_features(n, carry):
         for t in range(4):
@@ -467,7 +481,9 @@
 
     def skeleton_rows(n, carry):
         for t in range(PER // 2):
-            skel_rows[n * (PER // 2) + t] = source_rows(gather1[n, 2 + PER // 2 + t] - centre)
+            parts = [gather1[n, 2 + PER // 2 + c, t : t + 1, :] for c in range(3)]
+            tile = jnp.concatenate(parts + [jnp.zeros((5, 128), F32)], axis=0)
+            skel_rows[n * (PER // 2) + t] = source_rows(tile - centre)
         return carry
 
     def far_matrix(lp, carry):
@@ -482,29 +498,26 @@
                 high, low = far_tiles(feat, rows)
                 far_high[l, :, 128 * p : 128 * (p + 1)] = high
                 far_low[l, :, 128 * p : 128 * (p + 1)] = low
-        return carry
-
-    def far_leaves(read):
-        def some(n, carry):
-            for q in range(2):
-                lp = 2 * n + q
-                parts = []
-                for side in range(2):
-                    l = 2 * lp + side
-                    count = far_count[l]
-                    cols = []
-                    for p in range(FARL // 2):
-                        s = 2 * p
-                        j1, j2 = far_leaf[l, s], far_leaf[l, s + 1]
-                        tile = joined(moved(read(j1), j1, 0), moved(read(j2), j2, 1))
-                        slot = s + jnp.where(low_lanes, 0, 1)
-                        cols.append(split2(jnp.where(slot < count, tile, 0.0)))
-                    c = jnp.concatenate(cols, axis=1)
-                    parts.append(dot_nt(far_high[l], c) + dot_nt(far_low[l], c))
-                local[lp] = -FACTOR * fold(jnp.concatenate(parts, axis=0).T)
-            return carry
-
-        lax.fori_loop(0, PER // 4, some, 0)
+        far_leaves(lp, lambda j: gather1[j >> 4, 2 + ((j >> 1) & 7)])
+        return carry
+
+    def far_leaves(n, read):
+        for q in range(2):
+            lp = 2 * n + q
+            parts = []
+            for side in range(2):
+                l = 2 * lp + side
+                count = far_count[l]
+                cols = []
+                for p in range(FARL // 2):
+                    s = 2 * p
+                    j1, j2 = far_leaf[l, s], far_leaf[l, s + 1]
+                    tile = joined(moved(read(j1), j1, 0), moved(read(j2), j2, 1))
+                    slot = s + jnp.where(low_lanes, 0, 1)
+                    cols.append(split2(jnp.where(slot < count, tile, 0.0)))
+                c = jnp.concatenate(cols, axis=1)
+                parts.append(dot_nt(far_high[l], c) + dot_nt(far_low[l], c))
+            local[lp] = -FACTOR * fold(jnp.concatenate(parts, axis=0).T)
 
     def upper_matrix(buffer):
         def read_mid(m):
@@ -562,7 +575,6 @@
 
     lax.fori_loop(0, GSIZE, skeleton_rows, 0)
     lax.fori_loop(0, PER // 4, far_matrix, 0)
-    far_leaves(lambda j: gather1[j >> 4, 2 + ((j >> 1) & 7)])
     wait_grp(all1, all_send, all_recv, 0)
     upper_matrix(all1)
     noise_value = noise[0]
@@ -594,7 +606,8 @@
     lax.fori_loop(PER // 8, PER // 4, first_leaves, 0)
     launch(halo_copies(halo2, 2, *right))
 
-    coefficients(lambda leaf: first[:, LEAF * leaf : LEAF * (leaf + 1)], gather2.at[i], 1)
+    coefficients(lambda leaf: first[:, LEAF * leaf : LEAF * (leaf + 1)], gather2.at[i], 0, mids2.at[i])
+    launch(leaf_copies(mids2, sum_send, sum_recv, 1))
     launch(leaf_copies(gather2, coef_send, coef_recv, 1))
     field_moments(PER)
     for copy in halo_copies(halo2, 1, *left) + halo_copies(halo2, 2, *right):
@@ -616,17 +629,24 @@
         multiply(n, 1)
         return carry
 
-    lax.fori_loop(0, PER // 2 - 2, near_again, 0)
-    wait_leaf(gather2, coef_send, coef_recv, 1)
+    lax.fori_loop(0, PER // 4, near_again, 0)
+    wait_leaf(mids2, sum_send, sum_recv, 1)
     group_top = jnp.zeros(tile_shape, F32)
     for p in range(GSIZE // 2):
-        one, two = gather2[2 * p, 0], gather2[2 * p + 1, 0]
+        one, two = mids2[2 * p], mids2[2 * p + 1]
         all2[g, p] = joined(one, pltpu.roll(two, RANK, 1))
         group_top += one + two
     all2[g, GSIZE // 2] = group_top
     launch(grp_copies(all2, all_send, all_recv, 1))
-    lax.fori_loop(PER // 2 - 2, PER // 2, near_again, 0)
-    far_leaves(lambda j: gather2[j >> 4, 1 + ((j >> 1) & 7)])
+    wait_leaf(gather2, coef_send, coef_recv, 1)
+
+    def near_and_far(n, carry):
+        multiply(PER // 4 + n, 0)
+        multiply(PER // 4 + n, 1)
+        far_leaves(n, lambda j: gather2[j >> 4, (j >> 1) & 7])
+        return carry
+
+    lax.fori_loop(0, PER // 4, near_and_far, 0)
     wait_grp(all2, all_send, all_recv, 1)
 
     def image_leaves(n, carry):
@@ -676,6 +696,7 @@
 def shards(*args):
     smem = pl.BlockSpec(memory_space=pltpu.SMEM)
     vmem = pl.BlockSpec(memory_space=pltpu.VMEM)
+    hbm = pl.BlockSpec(memory_space=pl.ANY)
     alphas, betas = tangent_tables()
     tables = (jnp.asarray(morton_table()), jnp.asarray(alphas), jnp.asarray(betas))
     out = jax.ShapeDtypeStruct((RHS, PER * LEAF), F32)
@@ -700,6 +721,7 @@
         buffer((3, 8, PER * LEAF)),
         buffer((GSIZE, TILES1) + tile),
         buffer((GSIZE, TILES2) + tile),
+        buffer((GSIZE,) + tile),
         buffer((GROUPS, GSIZE, 2) + tile),
         buffer((GROUPS, GSIZE // 2 + 1) + tile),
         buffer((GSIZE,) + tile),
@@ -721,21 +743,25 @@
         buffer((2, RANK, PER * RANK), BF),
         buffer((PER, 2 * RHS, LEAF)),
         buffer((PER // 2,) + tile),
+        buffer((RHS, PER * LEAF)),
+        buffer((PER, RANK, LEAF)),
+        buffer((PER, RANK, RANK)),
+        sems(3),
         sems(3, 2),
         sems(3, 2),
         sems(2, GSIZE),
         sems(2, GSIZE),
         sems(2, GROUPS),
         sems(2, GROUPS),
-        sems(1, GSIZE),
-        sems(1, GSIZE),
+        sems(2, GSIZE),
+        sems(2, GSIZE),
         sems(1, GROUPS),
         sems(1, GROUPS),
     ]
     first, image, step = pl.pallas_call(
         body,
         out_shape=(out, out, jax.ShapeDtypeStruct(tile, F32)),
-        in_specs=[vmem] * 9 + [smem] * 10,
+        in_specs=[hbm if n in (1, 6, 7) else vmem for n in range(9)] + [smem] * 10,
         out_specs=(vmem, vmem, vmem),
         scratch_shapes=scratch,
         compiler_params=pltpu.CompilerParams(

time: 90.9 us -> 87.4 us (0.961)
  Pallas kernels: 86.8 us -> 82.9 us
    pallas_call x1, Pallas kernels: 86.8 us -> 82.9 us  [shards(): pl.pallas_call(body, out_shape=(out, out, jax.ShapeDtypeStruct(tile, F32)...]
where the time goes in v4:
time: 87.4 us; the launch traced here: 86.8 us
  Pallas kernels  82.9 us (95%)
  other arithmetic  1.76 us (2%)
  between operations  1.31 us (1%)
    pallas_call x1, Pallas kernels, shards(): pl.pallas_call(body, out_shape=(out, out, jax.ShapeDtypeStruct(tile, F32)...  82.9 us
    sub x1, other arithmetic, shards(): return (args[2] + alpha * first, first - alpha * image)  1.76 us

profile of v4, /device:TPU:1, one launch (start us, length us, event | category | flops | bytes accessed | tf_op | source)
XLA Modules:
  0.0 86.8 jit_solution(12384968109327409522)
XLA Ops:
  1.3 0.0 copy-start
  1.3 82.9 %shard_map.194 = (f32[8,4096]{1,0:T(8,128)}, f32[8,4096]{1,0:T(8,128)}, f32[8,128]{1,0:T(8,128)}) custom-call(f32[3,4096]{1,0:T(4,128)} %points.1, f32[8,4096]{1,0:T(8,128)} %rhs_hbm.1, f32[8,4096]{1,0:T(8,128)} %start.1, f32[3,1024]{1,0:T(4,128)} %leaf_skel.1, f32[3,64]{1,0:T(4,128)} %mid_skel.1, f32[3,512]{1,0:T(4,128)} %top_skel.1, ...), custom_call_target="tpu_custom_call" | custom-call | tf_op jit(solution)/shard_map/pallas_call | solution.py:761
  84.2 0.0 copy-start.1
  84.2 0.7 copy-done.1
  84.9 0.1 slice_reduce_fusion
  85.0 0.0 copy-done
  85.0 1.8 %multiply_subtract_fusion = (f32[8,4096]{1,0:T(8,128)}, f32[8,4096]{1,0:T(8,128)}) fusion(f32[8,4096]{1,0:T(8,128)} %get-tuple-element.6, f32[8,4096]{1,0:T(8,128)} %get-tuple-element.7, f32[8]{0:T(128)S(1)} %slice_reduce_fusion, f32[8,4096]{1,0:T(8,128)S(1)} %copy-done), kind=kLoop, calls=%fused_computation | loop fusion | flops 131072 | bytes 655392 | tf_op jit(solution)/shard_map/sub | solution.py:772
Async XLA Ops:
  1.3 83.7 %copy-start = (f32[8,4096]{1,0:T(8,128)S(1)}, f32[8,4096]{1,0:T(8,128)}, u32[]{:S(2)}) copy-start(f32[8,4096]{1,0:T(8,128)} %start.1) | copy-start | bytes 393220
  84.2 0.7 copy-start.1

commit v5 on v4

--- a/solution.py
+++ b/solution.py
@@ -688,7 +688,7 @@
         total += sums2[k]
     total = total / (LEAVES * LEAF)
     alpha = total[:, 0:1] / (total[:, RANK : RANK + 1] + 1e-6)
-    step[...] = jnp.broadcast_to(alpha, (RHS, 128))
+    step[...] = jnp.broadcast_to(alpha, (RHS, PER * LEAF))
     for copy in pending:
         copy.wait_send()
 
@@ -760,7 +760,7 @@
     ]
     first, image, step = pl.pallas_call(
         body,
-        out_shape=(out, out, jax.ShapeDtypeStruct(tile, F32)),
+        out_shape=(out, out, out),
         in_specs=[hbm if n in (1, 6, 7) else vmem for n in range(9)] + [smem] * 10,
         out_specs=(vmem, vmem, vmem),
         scratch_shapes=scratch,
@@ -768,8 +768,7 @@
             collective_id=0, has_side_effects=True, vmem_limit_bytes=61 << 20
         ),
     )(*args, *tables)
-    alpha = step[:, 0:1]
-    return args[2] + alpha * first, first - alpha * image
+    return args[2] + step * first, first - step * image
 
 
 def solution(mesh):

time: 87.4 us -> 86.7 us (level)
  no operation moved by 1% of the time
where the time goes in v5:
time: 86.7 us; the launch traced here: 86 us
  Pallas kernels  83 us (96%)
  other arithmetic  1.76 us (2%)
  between operations  1.31 us (2%)
    pallas_call x1, Pallas kernels, shards(): pl.pallas_call(body, out_shape=(out, out, out), in_specs=[hbm if n in (1,...  83 us
    sub x1, other arithmetic, shards(): return (args[2] + step * first, first - step * image)  1.76 us

profile of v5, /device:TPU:1, one launch (start us, length us, event | category | flops | bytes accessed | tf_op | source)
XLA Modules:
  0.0 86.0 jit_solution(14242454466933549227)
XLA Ops:
  1.3 0.0 copy-start
  1.3 83.0 %shard_map.194 = (f32[8,4096]{1,0:T(8,128)}, f32[8,4096]{1,0:T(8,128)}, f32[8,4096]{1,0:T(8,128)}) custom-call(f32[3,4096]{1,0:T(4,128)} %points.1, f32[8,4096]{1,0:T(8,128)} %rhs_hbm.1, f32[8,4096]{1,0:T(8,128)} %start.1, f32[3,1024]{1,0:T(4,128)} %leaf_skel.1, f32[3,64]{1,0:T(4,128)} %mid_skel.1, f32[3,512]{1,0:T(4,128)} %top_skel.1, ...), custom_call_target="tpu_custom_call" | custom-call | tf_op jit(solution)/shard_map/pallas_call | solution.py:761
  84.3 0.0 copy-done
  84.3 1.8 %multiply_subtract_fusion = (f32[8,4096]{1,0:T(8,128)}, f32[8,4096]{1,0:T(8,128)}) fusion(f32[8,4096]{1,0:T(8,128)} %get-tuple-element.6, f32[8,4096]{1,0:T(8,128)} %get-tuple-element.5, f32[8,4096]{1,0:T(8,128)} %get-tuple-element.7, f32[8,4096]{1,0:T(8,128)S(1)} %copy-done), kind=kLoop, calls=%fused_computation | loop fusion | flops 131072 | bytes 786432 | tf_op jit(solution)/shard_map/sub | solution.py:771
Async XLA Ops:
  1.3 83.0 %copy-start = (f32[8,4096]{1,0:T(8,128)S(1)}, f32[8,4096]{1,0:T(8,128)}, u32[]{:S(2)}) copy-start(f32[8,4096]{1,0:T(8,128)} %start.1) | copy-start | bytes 393220

commit v6 on v5

--- a/solution.py
+++ b/solution.py
@@ -387,12 +387,11 @@
     tile = jnp.where(lax.rem(g, 2) == 0, tile, pltpu.roll(tile, RANK, 1))
     top_feat[...] = target_pieces(target_rows(tile - centre)).T.astype(BF)
 
-    def field_moments(first_leaf):
+    def field_moments(*first_leaves):
         lane8 = lax.broadcasted_iota(jnp.int32, (RHS, 8), 1)
 
         def some(n, carry):
-            for t in range(8):
-                leaf = first_leaf + 8 * n + t
+            for leaf in (first + 8 * n + t for t in range(8) for first in first_leaves):
                 r = fold(dot(field[leaf], wfeat[leaf]))
                 m = r[:, 0:8] + r[:, 8:16] + r[:, 32:40]
                 moments[leaf, 0] = m
@@ -416,8 +415,7 @@
         return carry
 
     lax.fori_loop(0, PER // 4, edge_features, 0)
-    field_moments(0)
-    field_moments(2 * PER)
+    field_moments(0, 2 * PER)
 
     shift = alphas[512]
     remainders = (remainder0, remainder1)
@@ -621,8 +619,7 @@
         return carry
 
     lax.fori_loop(0, PER // 4, edge_fields, 0)
-    field_moments(0)
-    field_moments(2 * PER)
+    field_moments(0, 2 * PER)
 
     def near_again(n, carry):
         multiply(n, 0)

time: 86.7 us -> 85.7 us (0.988)
  no operation moved by 1% of the time
where the time goes in v6:
time: 85.7 us; the launch traced here: 85.5 us
  Pallas kernels  82.4 us (96%)
  other arithmetic  1.76 us (2%)
  between operations  1.31 us (2%)
    pallas_call x1, Pallas kernels, shards(): pl.pallas_call(body, out_shape=(out, out, out), in_specs=[hbm if n in (1,...  82.4 us
    sub x1, other arithmetic, shards(): return (args[2] + step * first, first - step * image)  1.76 us

profile of v6, /device:TPU:1, one launch (start us, length us, event | category | flops | bytes accessed | tf_op | source)
XLA Modules:
  0.0 85.5 jit_solution(18226117235603301310)
XLA Ops:
  1.3 0.0 copy-start
  1.3 82.4 %shard_map.194 = (f32[8,4096]{1,0:T(8,128)}, f32[8,4096]{1,0:T(8,128)}, f32[8,4096]{1,0:T(8,128)}) custom-call(f32[3,4096]{1,0:T(4,128)} %points.1, f32[8,4096]{1,0:T(8,128)} %rhs_hbm.1, f32[8,4096]{1,0:T(8,128)} %start.1, f32[3,1024]{1,0:T(4,128)} %leaf_skel.1, f32[3,64]{1,0:T(4,128)} %mid_skel.1, f32[3,512]{1,0:T(4,128)} %top_skel.1, ...), custom_call_target="tpu_custom_call" | custom-call | tf_op jit(solution)/shard_map/pallas_call | solution.py:758
  83.7 0.0 copy-done
  83.7 1.8 %multiply_subtract_fusion = (f32[8,4096]{1,0:T(8,128)}, f32[8,4096]{1,0:T(8,128)}) fusion(f32[8,4096]{1,0:T(8,128)} %get-tuple-element.6, f32[8,4096]{1,0:T(8,128)} %get-tuple-element.5, f32[8,4096]{1,0:T(8,128)} %get-tuple-element.7, f32[8,4096]{1,0:T(8,128)S(1)} %copy-done), kind=kLoop, calls=%fused_computation | loop fusion | flops 131072 | bytes 786432 | tf_op jit(solution)/shard_map/sub | solution.py:768
Async XLA Ops:
  1.3 82.4 %copy-start = (f32[8,4096]{1,0:T(8,128)S(1)}, f32[8,4096]{1,0:T(8,128)}, u32[]{:S(2)}) copy-start(f32[8,4096]{1,0:T(8,128)} %start.1) | copy-start | bytes 393220
